TPU v7x, 32 devices: a whole 2x2x4 slice. The times are simulated.
32 devices in a mesh: sec: 2 (over x), ty: 4 (over y, core), tx: 4 (over z).
Axes of the slice: x: 2, y: 2, z: 4, core: 2. Of those that a mesh axis runs over, the one named last changes fastest.
Arguments:
- descriptors: bfloat16 [2, 4, 4, 1024, 128], P('sec', 'ty', 'tx'), may hold values from -4 to 4, as said below
- positions: bfloat16 [2, 4, 4, 2, 1024], P('sec', 'ty', 'tx'), may hold values from -1 to 1
- vertex_ids: int32 [2, 4, 4, 1024], P('sec', 'ty', 'tx'), may hold values from 0 to 262143, as said below
- candidate_blocks: int32 [2, 4, 4, 32], P('sec', 'ty', 'tx'), may hold values from 0 to 127, as said below
- candidate_count: int32 [2, 4, 4], P('sec', 'ty', 'tx'), may hold values from 8 to 32, as said below
- displacement: float32 [2, 2, 512, 512], P('sec', None, 'ty', 'tx'), may hold values from -3 to 3
- stiffness: float32 [2, 512, 512], P('sec', 'ty', 'tx'), may hold values from 0.25 to 4
Outputs:
- relaxed: float32 [2, 2, 512, 512], P('sec', None, 'ty', 'tx')
Inputs may be any that keep to these rules, and one draw needn't show every extreme that they name: `descriptors`: descriptor entries stay within the range. `candidate_blocks`: A list names distinct blocks tile * 8 + j of the next section; among its live entries at most 4 blocks come from any one tile, and some list has 4 live blocks of one tile. `candidate_count`: some tile has all 32 entries live. `vertex_ids`: ids follow the vertex numbering of the steps, anywhere in the section.
All inputs are finite; a program needn't handle non-finite values.
Results may differ from a plain program's by a relative error of at most 0.0019.
Values may be sent and summed in bfloat16 or wider, within the bound.
No kernel may reach another device: no remote copies, remote signals or barrier semaphores. Data moves between devices by JAX's collectives and lax.ppermute only.
A program may use at most 192 MiB of HBM per device.

v0:
```python
import functools
import math

import jax
import jax.numpy as jnp
from jax import lax
from jax.experimental import pallas as pl
from jax.experimental.pallas import tpu as pltpu
from jax.sharding import PartitionSpec as P

BLK = 128
ITERS = 4
LANES = 128
PLACE_ROWS = 16
GROUP = 2
ROUND = 8
BASE = 256
DIGITS = 3
VMEM_BYTES = 24 * 1024 * 1024

spring_sec = 0.5
spring_match = 1.0
relax_rate = 0.8


def passed_along(value, axis, by):
    devices = lax.axis_size(axis)
    pairs = [(i, i + by) for i in range(devices) if 0 <= i + by < devices]
    return lax.ppermute(value, axis, pairs)


def exchanged(value, axes):
    return lax.all_to_all(value, axes, split_axis=0, concat_axis=0, tiled=True)


def spread(value, axes):
    copies = jnp.broadcast_to(value[None], (lax.axis_size(axes),) + value.shape)
    return exchanged(copies, axes)


def nt_dot(a, b):
    return lax.dot_general(a, b, (((1,), (1,)), ((), ())), preferred_element_type=jnp.float32)


def in_vmem(count):
    return [pl.BlockSpec(memory_space=pltpu.VMEM)] * count


def in_smem():
    return pl.BlockSpec(memory_space=pltpu.SMEM)


def match_kernel(scale, plan, last, at_ref, *refs):
    tile_rows = max(i for i, _ in plan) + 1
    key_tiles = max(max(among) for _, among in plan if among) + 1
    query_refs, refs = refs[:tile_rows], refs[tile_rows:]
    key_refs, refs = refs[:key_tiles], refs[key_tiles:]
    if last:
        before_ref, edge_ref, out_ref = refs[:3]
        refs = refs[3:]
    else:
        (out_ref,) = refs[:1]
        refs = refs[1:]
    query_buf, key_buf, place_buf, state_buf, list_buf = refs
    point_total = state_buf.shape[2]
    all_tiles, key_rows = key_buf.shape[:2]
    part = key_rows // BLK
    total = all_tiles * part
    own_row, share, shares = at_ref[3], at_ref[4], at_ref[5]
    rows_at, cols_at = 6, 6 + query_buf.shape[0]

    number = 0
    for tile, among in plan:
        met = [at_ref[cols_at + i] for i in among]
        listed = query_refs[tile][pl.ds(point_total, PLACE_ROWS), :]
        listed = listed.astype(jnp.float32).astype(jnp.int32)
        here = listed[0:1] == own_row * shares + share
        for low in range(0, total, 16):
            place = listed[1:2] - low
            bits = jnp.where(here & (place >= 0) & (place < 16), 1 << jnp.clip(place, 0, 15), 0)
            bits = jnp.sum(bits)
            for i in range(low, min(low + 16, total)):
                allowed = functools.reduce(jnp.logical_or, [col == i // part for col in met])
                list_buf[number] = tile * total + i
                number = number + jnp.where(allowed, (bits >> (i - low)) & 1, 0)
        list_buf[number] = -1
        number = number + lax.rem(number, 2)
    for i in range(2 * GROUP):
        list_buf[number + i] = -1
    groups = lax.div(number + 2 * GROUP - 1, 2 * GROUP)

    row_at = lax.broadcasted_iota(jnp.int32, (PLACE_ROWS, LANES), 0)
    ids = []
    for tile, key_ref in enumerate(key_refs):
        col = at_ref[cols_at + tile]
        key_buf[col] = key_ref[pl.ds(0, key_rows), :]
        rest = key_ref[pl.ds(key_rows, key_ref.shape[0] - key_rows), :].astype(jnp.float32)
        for j in range(part):
            x, y = rest[j : j + 1, :], rest[part + j : part + j + 1, :]
            stacked = jnp.where(
                row_at == 0, x, jnp.where(row_at == 1, y, jnp.where(row_at == 2, 1.0, 0.0))
            )
            place_buf[col * part + j] = stacked.astype(jnp.bfloat16)
        digits = [rest[(2 + i) * part : (3 + i) * part] for i in range(DIGITS)]
        ids.append(sum(digit * float(BASE**i) for i, digit in enumerate(digits)))
    for tile, query_ref in enumerate(query_refs):
        query_buf[tile] = query_ref[pl.ds(0, point_total), :]

    state_row = lax.broadcasted_iota(jnp.int32, state_buf.shape[1:], 0)
    for tile in range(tile_rows):
        if last and tile < before_ref.shape[0]:
            state_buf[tile] = before_ref[tile]
        else:
            state_buf[tile] = jnp.where(state_row == 3, -1e30, 0.0)

    def item(at):
        codes = [list_buf[2 * at + i] for i in range(2)]
        tile = lax.div(jnp.maximum(codes[0], 0), total)
        keys, places = [], []
        for i, code in enumerate(codes):
            block = lax.rem(jnp.maximum(jnp.where(code >= 0, code, codes[0]), 0), total)
            block = jnp.where(codes[0] >= 0, block, at_ref[cols_at] * part)
            start = pl.multiple_of(lax.rem(block, part) * BLK, BLK)
            keys.append(key_buf[lax.div(block, part), pl.ds(start, BLK), :])
            kept = jnp.where(code >= 0, 1.0, 0.0).astype(jnp.bfloat16)
            places.append(place_buf[block] * kept)
        return tile, codes[0] >= 0, jnp.concatenate(keys, axis=0), jnp.concatenate(places, axis=1)

    @pl.loop(0, groups)
    def _(group):
        items = [item(group * GROUP + i) for i in range(GROUP)]
        scores = [nt_dot(keys, query_buf[tile]) * scale for tile, _, keys, _ in items]
        tops = [jnp.max(score, axis=0, keepdims=True) for score in scores]
        weights = [jnp.exp2(s - top).astype(jnp.bfloat16) for s, top in zip(scores, tops)]
        sums = [
            jnp.dot(place, weight, preferred_element_type=jnp.float32)[0:8]
            for (_, _, _, place), weight in zip(items, weights)
        ]
        for (tile, live, _, _), top, added in zip(items, tops, sums):
            top = jnp.where(live, top, -1e30)
            state = state_buf[tile]
            before = state[3:4, :]
            both = jnp.maximum(before, top)
            state = state * jnp.exp2(before - both) + added * jnp.exp2(top - both)
            state_buf[tile] = jnp.where(state_row == 3, both, state)

    if not last:
        out_ref[...] = state_buf[pl.ds(0, tile_rows)]
        return
    edge_rows = edge_ref.shape[1]
    for tile in range(tile_rows):
        to = at_ref[rows_at + tile]
        for row in range(point_total // LANES):
            lanes = pl.ds(row * LANES, LANES)
            for place, held in enumerate((3, 2, 0, 1)):
                out_ref[row // part, to, pl.ds(place * part + row % part, 1), :] = state_buf[
                    tile, pl.ds(held, 1), lanes
                ]
        for share in range(out_ref.shape[0]):
            out_ref[share, tile, pl.ds(4 * part, key_tiles * part), :] = jnp.concatenate(ids, axis=0)
            out_ref[share, tile, pl.ds((4 + key_tiles) * part, edge_rows), :] = jnp.where(
                tile > own_row, edge_ref[1], jnp.where(tile < own_row, edge_ref[0], edge_ref[2])
            )


def match(at, queries, keys, edges, score_factor, shares, part):
    tile_rows, key_tiles = len(queries), len(keys)
    point_total, width = queries[0].shape[0] - PLACE_ROWS, queries[0].shape[1]
    total = key_tiles * part

    def call(plan, out_shape, *more):
        many_rows = max(i for i, _ in plan) + 1
        many_keys = max(max(among) for _, among in plan if among) + 1
        scores = sum(len(among) for _, among in plan) * part * point_total * BLK
        return pl.pallas_call(
            functools.partial(
                match_kernel, score_factor * math.log2(math.e), plan, len(more) > 0
            ),
            out_shape=jax.ShapeDtypeStruct(out_shape, jnp.float32),
            in_specs=[in_smem()] + in_vmem(many_rows + many_keys + len(more)),
            out_specs=pl.BlockSpec(memory_space=pltpu.VMEM),
            scratch_shapes=[
                pltpu.VMEM((tile_rows, point_total, width), jnp.bfloat16),
                pltpu.VMEM((key_tiles, part * BLK, width), jnp.bfloat16),
                pltpu.VMEM((total, PLACE_ROWS, LANES), jnp.bfloat16),
                pltpu.VMEM((tile_rows, 8, point_total), jnp.float32),
                pltpu.SMEM((tile_rows * (total + 1) + 2 * GROUP + 1,), jnp.int32),
            ],
            compiler_params=pltpu.CompilerParams(vmem_limit_bytes=VMEM_BYTES),
            cost_estimate=pl.CostEstimate(
                flops=scores * width, bytes_accessed=4 * scores // BLK, transcendentals=scores // 4
            ),
            name="match_rest" if more else "match",
        )(at, *queries[:many_rows], *keys[:many_keys], *more)

    there = [
        [i for i in range(n) if i.bit_count() < 2 or n & (n - 1)] for n in (tile_rows, key_tiles)
    ]
    first = [(i, tuple(there[1])) for i in there[0]]
    rest = [(i, tuple(j for j in range(key_tiles) if j not in there[1])) for i in there[0]]
    rest = [v for v in rest if v[1]]
    rest += [(i, tuple(range(key_tiles))) for i in range(tile_rows) if i not in there[0]]
    if rest:
        state = call(first, (len(first), 8, point_total))
    else:
        rest, row = first, jnp.arange(8)[None, :, None]
        state = jnp.where(row == 3, -1e30, jnp.zeros((tile_rows, 8, point_total), jnp.float32))
    shape = (shares, tile_rows, (4 + key_tiles) * part + edges.shape[1], LANES)
    return call(rest, shape, state, edges)


def combine_kernel(parts_ref, place_ref, out_ref):
    parts = parts_ref.shape[0]
    rows = place_ref.shape[0] // 2
    tops = [parts_ref[i, 0:rows, :] for i in range(parts)]
    top = functools.reduce(jnp.maximum, tops)
    total = x = y = jnp.zeros_like(top)
    for i in range(parts):
        gain = jnp.exp2(tops[i] - top)
        total += gain * parts_ref[i, rows : 2 * rows, :]
        x += gain * parts_ref[i, 2 * rows : 3 * rows, :]
        y += gain * parts_ref[i, 3 * rows : 4 * rows, :]
    pull = jnp.concatenate([x / total, y / total], axis=0) - place_ref[...]
    for i in range(out_ref.shape[0]):
        out_ref[i] = pull


def combine(parts, place, copies):
    return pl.pallas_call(
        combine_kernel,
        out_shape=jax.ShapeDtypeStruct((copies,) + place.shape, jnp.float32),
        in_specs=in_vmem(2),
        out_specs=pl.BlockSpec(memory_space=pltpu.VMEM),
        compiler_params=pltpu.CompilerParams(vmem_limit_bytes=VMEM_BYTES),
        name="combine",
    )(parts, place)


def one_hot(at, length, limits):
    count = at.shape[1]
    parts, done = [], 0
    for low, high in limits:
        spot = lax.broadcasted_iota(jnp.int32, (high - low, count), 0) + low
        if low > done:
            parts.append(jnp.zeros((low - done, count), jnp.bfloat16))
        parts.append(jnp.where(spot == at, 1.0, 0.0).astype(jnp.bfloat16))
        done = high
    if length > done:
        parts.append(jnp.zeros((length - done, count), jnp.bfloat16))
    return jnp.concatenate(parts, axis=0)


def flat(value):
    return jnp.concatenate([value[i : i + 1, :] for i in range(value.shape[0])], axis=1)


def hits(side, halo, tall, wide, row, col):
    up = lambda n: -(-n // 16) * 16
    limits = ((0, up(side + halo)), (wide - up(halo), wide))
    return one_hot(flat(row), tall, ((0, tall),)), one_hot(flat(col), wide, limits)


def ranked(rank, row, values):
    sums = [0.0] * len(values)
    for tile in range(rank.shape[0]):
        here = rank[tile] == row
        sums = [total + jnp.where(here, v[tile], 0.0) for total, v in zip(sums, values)]
    return [jnp.sum(total, axis=0, keepdims=True) for total in sums]


def spots_kernel(
    side, halo, key_tiles, at_ref, parts_ref, rounds_ref, rank_ref, spot_ref, count_ref, hit_buf
):
    shares, tile_rows, _, _ = parts_ref.shape
    count = rank_ref.shape[1]
    rows = count // shares
    tall, wide = count_ref.shape

    def folded(at, length):
        return jnp.where(
            (at >= 0) & (at < side + halo), at, jnp.where((at < 0) & (at >= -halo), at + length, -1)
        )

    number = jnp.zeros((1, LANES), jnp.int32)
    point_row = lax.broadcasted_iota(jnp.int32, (count, LANES), 0)
    for i in range(tile_rows):
        for j in range(key_tiles):
            ids = jnp.concatenate(
                [parts_ref[k, i, pl.ds((4 + j) * rows, rows), :] for k in range(shares)], axis=0
            ).astype(jnp.int32)
            tile_of = lax.div(ids, side * side)
            within = lax.rem(ids, side * side)
            row = lax.div(tile_of, key_tiles) * side + lax.div(within, side) - at_ref[0]
            col = lax.rem(tile_of, key_tiles) * side + lax.rem(within, side) - at_ref[1]
            row, col = folded(row, side + 2 * halo), folded(col, wide)
            here = (row >= 0) & (col >= 0)
            hit = here.astype(jnp.int32)
            by = 1
            while by < count:
                hit = hit + jnp.where(point_row >= by, pltpu.roll(hit, by, 0), 0)
                by *= 2
            tile = i * key_tiles + at_ref[6 + tile_rows + j]
            rank_ref[tile] = jnp.where(here, number + hit - 1, -1)
            hit_buf[0, tile] = row.astype(jnp.float32) + 1.0
            hit_buf[1, tile] = col.astype(jnp.float32) + 1.0
            number = number + hit[count - 1 : count, :]
    rounds = lax.div(jnp.max(number) + ROUND - 1, ROUND)
    rounds_ref[0] = rounds
    count_ref[...] = jnp.zeros_like(count_ref)

    @pl.loop(0, rounds)
    def _(k):
        found = [ranked(rank_ref, k * ROUND + r, (hit_buf.at[0], hit_buf.at[1])) for r in range(ROUND)]
        row, col = (jnp.concatenate(v, axis=0).astype(jnp.int32) - 1 for v in zip(*found))
        spot_ref[k, 0] = row
        spot_ref[k, 1] = col
        row_hit, col_hit = hits(side, halo, tall, wide, row, col)
        count_ref[...] += nt_dot(row_hit, col_hit)


def spots(side, halo, key_tiles, wide, at, parts, rows):
    tall = -(-(side + 2 * halo) // 16) * 16
    count = parts.shape[0] * rows
    tiles = parts.shape[1] * key_tiles
    rounds = -(-tiles * count // ROUND)
    return pl.pallas_call(
        functools.partial(spots_kernel, side, halo, key_tiles),
        out_shape=(
            jax.ShapeDtypeStruct((1,), jnp.int32),
            jax.ShapeDtypeStruct((tiles, count, LANES), jnp.int32),
            jax.ShapeDtypeStruct((rounds, 2, ROUND, LANES), jnp.int32),
            jax.ShapeDtypeStruct((tall, wide), jnp.float32),
        ),
        in_specs=[in_smem()] + in_vmem(1),
        out_specs=(in_smem(),) + (pl.BlockSpec(memory_space=pltpu.VMEM),) * 3,
        scratch_shapes=[pltpu.VMEM((2, tiles, count, LANES), jnp.float32)],
        compiler_params=pltpu.CompilerParams(vmem_limit_bytes=VMEM_BYTES),
        cost_estimate=pl.CostEstimate(
            flops=8 * tall * ROUND * LANES * wide,
            bytes_accessed=8 * parts.size,
            transcendentals=0,
        ),
        name="spots",
    )(at, parts)


def vertex_sums(side, halo, rounds_ref, rank_ref, spot_ref, points_ref, sum_ref, point_buf):
    _, tall, wide = sum_ref.shape
    shares, tiles, both_rows, _ = points_ref.shape
    rows = both_rows // 2
    sum_ref[...] = jnp.zeros_like(sum_ref)
    for tile in range(tiles):
        for share in range(shares):
            for c in range(2):
                point_buf[c, tile, pl.ds(share * rows, rows), :] = points_ref[
                    share, tile, pl.ds(c * rows, rows), :
                ]

    @pl.loop(0, rounds_ref[0])
    def _(k):
        found = [
            ranked(rank_ref, k * ROUND + r, (point_buf.at[0], point_buf.at[1])) for r in range(ROUND)
        ]
        _, col_hit = hits(side, halo, tall, wide, spot_ref[k, 0], spot_ref[k, 1])
        row = flat(spot_ref[k, 0])
        row_hit = lax.broadcasted_iota(jnp.int32, (tall, row.shape[1]), 0) == row
        parts = []
        for value in zip(*found):
            value = jnp.concatenate(value, axis=1)
            high = value.astype(jnp.bfloat16).astype(jnp.float32)
            for part in (high, value - high):
                parts.append(jnp.where(row_hit, part, 0.0).astype(jnp.bfloat16))
        summed = nt_dot(jnp.concatenate(parts, axis=0), col_hit)
        sum_ref[0] += summed[0:tall] + summed[tall : 2 * tall]
        sum_ref[1] += summed[2 * tall : 3 * tall] + summed[3 * tall :]


def sums_kernel(side, halo, rounds_ref, rank_ref, spot_ref, points_ref, out_ref, sum_ref, point_buf):
    vertex_sums(side, halo, rounds_ref, rank_ref, spot_ref, points_ref, sum_ref, point_buf)
    out_ref[...] = sum_ref[:, pl.ds(0, out_ref.shape[1]), :]


def relax_kernel(
    side,
    halo,
    extent,
    at_ref,
    rounds_ref,
    rank_ref,
    spot_ref,
    count_ref,
    points_ref,
    mesh_ref,
    out_ref,
    sum_ref,
    point_buf,
):
    vertex_sums(side, halo, rounds_ref, rank_ref, spot_ref, points_ref, sum_ref, point_buf)
    span = side + 2 * halo
    wide = sum_ref.shape[2]
    shape = (span, wide)
    row = lax.broadcasted_iota(jnp.int32, shape, 0)
    col = lax.broadcasted_iota(jnp.int32, shape, 1)
    row = jnp.where(row < side + halo, row, row - span) + at_ref[0]
    col = jnp.where(col < side + halo, col, col - wide) + at_ref[1]
    inside = (row >= 0) & (row < extent[0]) & (col >= 0) & (col < extent[1])
    own_pulled = (at_ref[2] == 0).astype(jnp.float32)
    linked = 1.0
    matched = count_ref[pl.ds(0, span), :]
    moving, gains, has, step = [], [], [], []
    for part, pulled in enumerate((own_pulled, 1.0 - own_pulled)):
        gain = mesh_ref[part * 3 + 2]
        diagonal = 4.0 * gain + spring_sec * linked + spring_match * matched * pulled
        gains.append(gain)
        has.append(matched * pulled)
        step.append(jnp.where(inside, relax_rate / diagonal, 0.0))
        moving.append(
            [(mesh_ref[part * 3 + c], sum_ref[c, pl.ds(0, span), :] * pulled) for c in range(2)]
        )
    for sweep in range(ITERS):
        later = []
        for part in range(2):
            row_of = []
            for c in range(2):
                u, pulled = moving[part][c]
                other = moving[1 - part][c][0]
                laplace = (
                    pltpu.roll(u, 1, 0)
                    + pltpu.roll(u, span - 1, 0)
                    + pltpu.roll(u, 1, 1)
                    + pltpu.roll(u, wide - 1, 1)
                    - 4.0 * u
                )
                force = (
                    gains[part] * laplace
                    + spring_sec * (other - linked * u)
                    + spring_match * (pulled - has[part] * u)
                )
                row_of.append((u + step[part] * force, pulled))
            later.append(row_of)
        moving = later
    for c in range(2):
        out_ref[c] = moving[0][c][0][0:side, 0:side]


def col_edges(value, halo):
    after = passed_along(value[:, :, :halo].swapaxes(1, 2), "tx", -1)
    before = passed_along(value[:, :, value.shape[2] - halo :].swapaxes(1, 2), "tx", 1)
    return jnp.concatenate([after, before], axis=1)


def sweeps(moving, gains, sums, number, at, side, halo, extent):
    sections = lax.axis_size("sec")
    sec_index = at[2]
    has_next = (sec_index < sections - 1).astype(jnp.float32)
    linked = (sec_index > 0).astype(jnp.float32) + has_next
    pulled, matched = sums * has_next, number * has_next
    span, wide = moving.shape[1:]
    row = jnp.arange(span)[:, None]
    col = jnp.arange(wide)[None, :]
    row = jnp.where(row < side + halo, row, row - span) + at[0]
    col = jnp.where(col < side + halo, col, col - wide) + at[1]
    inside = (row >= 0) & (row < extent[0]) & (col >= 0) & (col < extent[1])
    diagonal = 4.0 * gains + spring_sec * linked + spring_match * matched
    step = jnp.where(inside, relax_rate / jnp.where(inside, diagonal, 1.0), 0.0)
    for sweep in range(ITERS):
        lower_sec = passed_along(moving, "sec", 1)
        upper_sec = passed_along(moving, "sec", -1)
        laplace = (
            jnp.roll(moving, 1, 1)
            + jnp.roll(moving, -1, 1)
            + jnp.roll(moving, 1, 2)
            + jnp.roll(moving, -1, 2)
            - 4.0 * moving
        )
        force = (
            gains * laplace
            + spring_sec * (lower_sec + upper_sec - linked * moving)
            + spring_match * (pulled - matched * moving)
        )
        moving = moving + step * force
    return moving[:, :side, :side]


def pack_kernel(
    shares,
    tile_cols,
    desc_hbm,
    place_hbm,
    ids_hbm,
    list_hbm,
    count_hbm,
    first_ref,
    second_ref,
    place_ref,
    ids_ref,
    list_ref,
    count_ref,
    last_ref,
    sems,
):
    half = second_ref.shape[0]
    copies = [
        pltpu.make_async_copy(source, target, sems.at[i])
        for i, (source, target) in enumerate(
            (
                (place_hbm, place_ref),
                (ids_hbm, ids_ref),
                (list_hbm, list_ref),
                (count_hbm, count_ref),
                (desc_hbm.at[pl.ds(0, half), :], first_ref.at[pl.ds(0, half), :]),
                (desc_hbm.at[pl.ds(half, half), :], second_ref),
            )
        )
    ]
    for copy in copies:
        copy.start()
    for copy in copies[:4]:
        copy.wait()

    def cut(row):
        return [row[:, i : i + LANES] for i in range(0, row.shape[1], LANES)]

    place, ids, blocks = place_ref[...].astype(jnp.float32), ids_ref[...], list_ref[...]
    rows = cut(place[0:1]) + cut(place[1:2])
    for i in range(DIGITS):
        digit = lax.rem(lax.div(ids, BASE**i), BASE)
        rows += cut(digit.astype(jnp.float32))
    per_tile = place.shape[1] // BLK
    part = per_tile // shares
    tile, within = lax.div(blocks, per_tile), lax.rem(blocks, per_tile)
    device = lax.div(tile, tile_cols) * shares + lax.div(within, part)
    spot = lax.rem(tile, tile_cols) * part + lax.rem(within, part)
    live = lax.broadcasted_iota(jnp.int32, blocks.shape, 1) < count_ref[0, 0]
    last_ref[...] = jnp.full_like(last_ref, BASE - 1.0)
    last_ref[0:1, 0 : blocks.shape[1]] = jnp.where(live, device, BASE - 1).astype(jnp.float32)
    last_ref[1:2, 0 : blocks.shape[1]] = spot.astype(jnp.float32)
    count = first_ref.shape[0] - half
    gap = jnp.zeros((count - len(rows) - PLACE_ROWS, LANES), jnp.float32)
    rows += ([gap] if gap.shape[0] else []) + [last_ref[...]]
    first_ref[pl.ds(half, count), :] = jnp.concatenate(rows, axis=0).astype(jnp.bfloat16)
    for copy in copies[4:]:
        copy.wait()


def pack(desc, place, ids, blocks, count, shares, tile_cols):
    points, width = desc.shape
    half = points // 2
    rows = -(-(2 + DIGITS) * (points // LANES) // 16) * 16 + PLACE_ROWS
    return pl.pallas_call(
        functools.partial(pack_kernel, shares, tile_cols),
        out_shape=(
            jax.ShapeDtypeStruct((half + rows, width), jnp.bfloat16),
            jax.ShapeDtypeStruct((half, width), jnp.bfloat16),
        ),
        in_specs=[pl.BlockSpec(memory_space=pltpu.HBM)] * 5,
        out_specs=(pl.BlockSpec(memory_space=pltpu.VMEM),) * 2,
        scratch_shapes=[
            pltpu.VMEM(place.shape, place.dtype),
            pltpu.VMEM(ids.shape, ids.dtype),
            pltpu.VMEM(blocks.shape, blocks.dtype),
            pltpu.SMEM(count.shape, count.dtype),
            pltpu.VMEM((PLACE_ROWS, LANES), jnp.float32),
            pltpu.SemaphoreType.DMA((6,)),
        ],
        name="pack",
    )(desc, place, ids, blocks, count)


def turns(axis):
    devices, here = lax.axis_size(axis), lax.axis_index(axis)
    if devices & (devices - 1):
        pairs = [[(i, (i + j) % devices) for i in range(devices)] for j in range(1, devices)]
        return pairs, jnp.mod(here - jnp.arange(devices), devices)
    pairs = [[(i, i ^ j) for i in range(devices)] for j in range(1, devices)]
    return pairs, here ^ jnp.arange(devices)


def key_kernel(shares, sec_ref, first_ref, second_ref, other_ref, key_ref, place_ref):
    half = second_ref.shape[0]
    per_tile = 2 * half // LANES
    part = per_tile // shares
    own, other = first_ref, first_ref
    if shares == 2:
        other = other_ref
    at_first = sec_ref[0] == 0

    def rest(ref, share):
        rows = ref[pl.ds(half, (2 + DIGITS) * per_tile), :].astype(jnp.float32)
        kept = [
            rows[i * per_tile + share * part : i * per_tile + (share + 1) * part]
            for i in range(2 + DIGITS)
        ]
        return jnp.concatenate(kept[:2], axis=0), kept[2:]

    if shares == 2:
        keys = jnp.where(at_first, other[pl.ds(0, half), :], second_ref[...])
        key_ref[pl.ds(0, half), :] = keys
        (own_0, ids_0), (own_1, _) = rest(own, 0), rest(own, 1)
        (other_0, _), (other_1, ids_1) = rest(other, 0), rest(other, 1)
        key_place = jnp.where(at_first, other_0, own_1)
        place_ref[...] = jnp.where(at_first, own_0, other_1)
        ids = [jnp.where(at_first, a, b) for a, b in zip(ids_0, ids_1)]
    else:
        key_ref[pl.ds(0, half), :] = own[pl.ds(0, half), :]
        key_ref[pl.ds(half, half), :] = second_ref[...]
        key_place, _ = rest(own, 0)
        place_ref[...], ids = rest(other_ref, 0)
    done = part * BLK
    filler = jnp.zeros((-(2 + DIGITS) * part % 16, LANES), jnp.float32)
    rows = [key_place] + ids + ([filler] if filler.shape[0] else [])
    key_ref[pl.ds(done, key_ref.shape[0] - done), :] = jnp.concatenate(rows, axis=0).astype(
        jnp.bfloat16
    )


def key_payload(sec, first_half, second_half, other, shares):
    half, width = second_half.shape
    part = 2 * half // LANES // shares
    rows = part * BLK + -(-(2 + DIGITS) * part // 16) * 16
    return pl.pallas_call(
        functools.partial(key_kernel, shares),
        out_shape=(
            jax.ShapeDtypeStruct((rows, width), jnp.bfloat16),
            jax.ShapeDtypeStruct((2 * part, LANES), jnp.float32),
        ),
        in_specs=[in_smem()] + in_vmem(3),
        out_specs=(pl.BlockSpec(memory_space=pltpu.VMEM),) * 2,
        compiler_params=pltpu.CompilerParams(vmem_limit_bytes=VMEM_BYTES),
        name="key_payload",
    )(sec, first_half, second_half, other)


def query_kernel(shares, sec_ref, first_ref, second_ref, other_ref, came_ref, out_ref):
    half = second_ref.shape[0]
    last = first_ref.shape[0] - PLACE_ROWS

    def chosen(own, other):
        return jnp.where(sec_ref[0] == 0, own, other) if shares == 2 else other

    for target, rows in ((0, pl.ds(0, half)), (2 * half, pl.ds(last, PLACE_ROWS))):
        out_ref[pl.ds(target, rows.size), :] = chosen(first_ref[rows, :], other_ref[rows, :])
    out_ref[pl.ds(half, half), :] = chosen(second_ref[...], came_ref[...])


def query_payload(sec, first_half, second_half, other, came, shares):
    half, width = second_half.shape
    return pl.pallas_call(
        functools.partial(query_kernel, shares),
        out_shape=jax.ShapeDtypeStruct((2 * half + PLACE_ROWS, width), jnp.bfloat16),
        in_specs=[in_smem()] + in_vmem(4),
        out_specs=pl.BlockSpec(memory_space=pltpu.VMEM),
        compiler_params=pltpu.CompilerParams(vmem_limit_bytes=VMEM_BYTES),
        name="query_payload",
    )(sec, first_half, second_half, other, came)


def gathered(values, axes, beside):
    held, steps = [], []
    for value, axis in zip(values, axes):
        devices = lax.axis_size(axis)
        if devices & (devices - 1):
            moved = [lax.ppermute(value, axis, pairs) for pairs in turns(axis)[0]]
            held.append(dict(enumerate([value] + moved)))
            steps.append(0)
        else:
            held.append({0: value})
            steps.append(devices.bit_length() - 1)
    for step in range(1, max(steps) + 1):
        for i, axis in enumerate(axes):
            devices = lax.axis_size(axis)
            for at in range(devices - 1, 0, -1):
                if steps[i] and at.bit_count() == step:
                    by = at & -at
                    pairs = [(j, j ^ by) for j in range(devices)]
                    held[i][at] = lax.ppermute(held[i][at ^ by], axis, pairs)
        if step == 1:
            held, beside = lax.optimization_barrier((held, beside))
    return [[h[i] for i in range(len(h))] for h in held], beside


def per_device(
    descriptors, positions, vertex_ids, candidate_blocks, candidate_count, displacement, stiffness
):
    point_total, width = descriptors.shape[3:]
    per_tile = point_total // BLK
    tile_rows, tile_cols = lax.axis_size("ty"), lax.axis_size("tx")
    sections = lax.axis_size("sec")
    sec_index = lax.axis_index("sec")
    tiles = tile_rows * tile_cols
    side = displacement.shape[3]
    halo = ITERS
    span = side + 2 * halo
    wide = -(-span // LANES) * LANES
    cand = candidate_blocks.shape[3]
    shares = 2 if sections == 2 and per_tile % 2 == 0 else 1
    part = per_tile // shares
    key_rows = part * BLK

    first_half, second_half = pack(
        descriptors[0, 0, 0],
        positions[0, 0, 0],
        vertex_ids[0, 0],
        candidate_blocks[0, 0],
        candidate_count[0, 0][None],
        shares,
        tile_cols,
    )
    half = point_total // 2
    swap = [(i, 1 - i) for i in range(2)]

    sec = jnp.asarray(sec_index, jnp.int32)[None]
    own_mesh = jnp.concatenate([displacement[0], stiffness], axis=0)
    if shares == 2:
        share = sec_index
        other = lax.ppermute(first_half, "sec", swap)
    else:
        share = 0
        other = passed_along(first_half, "sec", 1)
    came = passed_along(second_half, "sec", 1)
    cols = col_edges(own_mesh, halo)
    key, place = key_payload(sec, first_half, second_half, other, shares)
    meshes = [own_mesh]
    if shares == 2:
        tied, key = lax.optimization_barrier((own_mesh, key))
        meshes.append(lax.ppermute(tied, "sec", swap))
    query = query_payload(sec, first_half, second_half, other, came, shares)
    (queries, keys), (cols, meshes) = gathered((query, key), ("ty", "tx"), (cols, meshes))
    at = jnp.concatenate(
        [
            jnp.stack([lax.axis_index("ty") * side, lax.axis_index("tx") * side, sec_index]),
            jnp.stack([lax.axis_index("ty"), jnp.asarray(share), jnp.asarray(shares)]),
            turns("ty")[1],
            turns("tx")[1],
        ]
    ).astype(jnp.int32)
    extent = (side * tile_rows, side * tile_cols)
    sum_shapes = [
        pltpu.VMEM((2, -(-span // 16) * 16, wide), jnp.float32),
        pltpu.VMEM((2, tiles, per_tile, LANES), jnp.float32),
    ]

    top, end = own_mesh[:, :halo], own_mesh[:, side - halo :]
    corners = [
        jnp.pad(v.swapaxes(1, 2), ((0, 0), (0, 0), (0, side - 2 * halo)))
        for v in (cols[:, :, :halo], cols[:, :, side - halo :])
    ]
    edges = [jnp.concatenate(v, axis=0) for v in ((top, corners[0]), (end, corners[1]))]
    edges = jnp.stack([v.reshape(-1, LANES) for v in edges + [cols]])
    parts = match(at, queries, keys, edges, 16.0 / width, shares, part)
    shape = parts.shape
    parts = exchanged(parts.reshape((-1,) + shape[2:]), ("sec", "ty") if shares == 2 else "ty")
    pulls = combine(parts, place, shares * tiles)
    parts, pulls, meshes = lax.optimization_barrier((parts, pulls, meshes))

    def edge_rows(by):
        near = lax.axis_index("ty") + by
        rows = parts.reshape(shape)[:, :, -edges.shape[1] :]
        rows = lax.dynamic_index_in_dim(rows, jnp.clip(near, 0, tile_rows - 1), 1, keepdims=False)
        rows = jnp.where((near >= 0) & (near < tile_rows), rows, 0.0)
        rows = rows.reshape(shares, 2, 3, halo, side)
        if shares == 2:
            rows = jnp.where(sec_index == 0, rows, rows[::-1])
        return [
            jnp.concatenate([rows[i, 0], rows[i, 1, :, :, : 2 * halo]], axis=2)
            for i in range(shares)
        ]

    after, before = edge_rows(1), edge_rows(-1)
    cols = [cols]
    if shares == 2:
        sent = parts.reshape(shape)[:, :, -edges.shape[1] :]
        sent = lax.dynamic_index_in_dim(sent, lax.axis_index("ty"), 1, keepdims=False)
        cols.append(jnp.where(sec_index == 0, sent[1], sent[0]).reshape(cols[0].shape))
    framed = []
    for i, mesh in enumerate(meshes):
        whole = jnp.concatenate([mesh, cols[i].swapaxes(1, 2)], axis=2)
        framed.append(jnp.concatenate([whole, after[i], before[i]], axis=1))
    framed = jnp.concatenate(framed, axis=0)
    gap = jnp.zeros(framed.shape[:2] + (wide - span,), framed.dtype)
    mesh_values = jnp.concatenate(
        [framed[:, :, : side + halo], gap, framed[:, :, side + halo :]], axis=2
    )
    if shares == 2:
        points = exchanged(pulls, ("sec", "ty", "tx"))
        rounds, rank, spot, number = spots(side, halo, tile_cols, wide, at, parts.reshape(shape), part)
        relaxed = pl.pallas_call(
            functools.partial(relax_kernel, side, halo, extent),
            out_shape=jax.ShapeDtypeStruct((2, side, side), jnp.float32),
            in_specs=[in_smem()] * 2 + in_vmem(5),
            out_specs=pl.BlockSpec(memory_space=pltpu.VMEM),
            scratch_shapes=sum_shapes,
            compiler_params=pltpu.CompilerParams(vmem_limit_bytes=VMEM_BYTES),
            name="relax",
        )(at, rounds, rank, spot, number, points.reshape(2, tiles, -1, LANES), mesh_values)
        return relaxed[None]

    points = passed_along(exchanged(pulls, ("ty", "tx")), "sec", -1)
    parts = passed_along(parts, "sec", -1)
    rounds, rank, spot, number = spots(side, halo, tile_cols, wide, at, parts[None], part)
    sums = pl.pallas_call(
        functools.partial(sums_kernel, side, halo),
        out_shape=jax.ShapeDtypeStruct((2, span, wide), jnp.float32),
        in_specs=[in_smem()] + in_vmem(3),
        out_specs=pl.BlockSpec(memory_space=pltpu.VMEM),
        scratch_shapes=sum_shapes,
        compiler_params=pltpu.CompilerParams(vmem_limit_bytes=VMEM_BYTES),
        name="sums",
    )(rounds, rank, spot, points[None])
    moving, gains = mesh_values[0:2], mesh_values[2]
    return sweeps(moving, gains, sums, number[:span], at, side, halo, extent)[None]


def solution(mesh):
    in_specs = (
        P("sec", "ty", "tx", None, None),
        P("sec", "ty", "tx", None, None),
        P("sec", "ty", "tx", None),
        P("sec", "ty", "tx", None),
        P("sec", "ty", "tx"),
        P("sec", None, "ty", "tx"),
        P("sec", "ty", "tx"),
    )
    out_specs = P("sec", None, "ty", "tx")
    return jax.shard_map(
        per_device, mesh=mesh, in_specs=in_specs, out_specs=out_specs, check_vma=False
    )
```

profile of v0, /device:TPU:0, one launch (start us, length us, event | category | flops | bytes accessed | tf_op | source)
XLA Modules:
  0.0 63.2 jit_solution(7936543090604221381)
XLA Ops:
  0.7 1.8 %pack.1 = (bf16[576,128]{1,0:T(8,128)(2,1)}, bf16[512,128]{1,0:T(8,128)(2,1)}) custom-call(bf16[1024,128]{1,0:T(8,128)(2,1)} %bitcast.58, bf16[2,1024]{1,0:T(2,128)(2,1)} %bitcast.64, s32[1,1024]{1,0:T(1,128)} %bitcast.65, s32[1,32]{1,0:T(1,128)} %bitcast.66, s32[1,1]{1,0:T(1,128)} %bitcast.48.count_hbm), custom_call_target="tpu_custom_call" | custom-call | tf_op jit(solution)/shard_map/pack/pallas_call | solution.py:550
  2.5 3.0 %collective-permute-start = (bf16[576,128]{1,0:T(8,128)(2,1)}, bf16[576,128]{1,0:T(8,128)(2,1)S(1)}, u32[]{:S(2)}, u32[]{:S(2)}) collective-permute-start(bf16[576,128]{1,0:T(8,128)(2,1)} %get-tuple-element.28.first_ref), channel_id=1, source_target_pairs={{0,16},{16,0},{1,17},{17,1},{2,18},{18,2},{3,19},{19,3},{4,20},{20... | collective-permute-start | bytes 442376 | tf_op jit(solution)/shard_map/ppermute | solution.py:716
  5.5 1.9 %collective-permute-start.1 = (bf16[512,128]{1,0:T(8,128)(2,1)}, bf16[512,128]{1,0:T(8,128)(2,1)S(1)}, u32[]{:S(2)}, u32[]{:S(2)}) collective-permute-start(bf16[512,128]{1,0:T(8,128)(2,1)} %get-tuple-element.29.second_ref), channel_id=1, source_target_pairs={{0,16},{1,17},{2,18},{3,19},{4,20},{5,21},{6,22},{7,23},{8,24},{9,... | collective-permute-start | bytes 393224 | tf_op jit(solution)/shard_map/ppermute | solution.py:29
  7.4 0.1 fusion.1
  7.6 1.3 %collective-permute-start.6 = (f32[3,4,128]{1,2,0:T(8,128)S(1)}, f32[3,4,128]{1,2,0:T(8,128)S(1)}, u32[]{:S(2)}, u32[]{:S(2)}) collective-permute-start(f32[3,4,128]{1,2,0:T(8,128)S(1)} %get-tuple-element.55), channel_id=1, source_target_pairs={{1,0},{2,1},{3,2},{5,4},{6,5},{7,6},{9,8},{10,9},{11,10},{13,12},{... | collective-permute-start | bytes 18440 | tf_op jit(solution)/shard_map/ppermute | solution.py:29
  8.9 4.6 %collective-permute-start.7 = (f32[3,4,128]{1,2,0:T(8,128)S(1)}, f32[3,4,128]{1,2,0:T(8,128)S(1)}, u32[]{:S(2)}, u32[]{:S(2)}) collective-permute-start(f32[3,4,128]{1,2,0:T(8,128)S(1)} %get-tuple-element.56), channel_id=1, source_target_pairs={{0,1},{1,2},{2,3},{4,5},{5,6},{6,7},{8,9},{9,10},{10,11},{12,13},{... | collective-permute-start | bytes 18440 | tf_op jit(solution)/shard_map/ppermute | solution.py:29
  13.6 0.8 %copy-done = bf16[576,128]{1,0:T(8,128)(2,1)S(1)} copy-done((bf16[576,128]{1,0:T(8,128)(2,1)S(1)}, bf16[576,128]{1,0:T(8,128)(2,1)}, u32[]{:S(2)}) %copy-start) | copy-done | bytes 147480
  14.6 2.0 %collective-permute-start.3 = (bf16[1040,128]{1,0:T(8,128)(2,1)S(1)}, bf16[1040,128]{1,0:T(8,128)(2,1)S(1)}, u32[]{:S(2)}, u32[]{:S(2)}) collective-permute-start(bf16[1040,128]{1,0:T(8,128)(2,1)S(1)} %query_payload.1.refs_0_), channel_id=1, source_target_pairs={{0,8},{4,12},{8,0},{12,4},{1,9},{5,13},{9,1},{13,5},{2,10},{6,14},... | collective-permute-start | bytes 798728 | tf_op jit(solution)/shard_map/ppermute | solution.py:676
  16.7 1.6 %collective-permute-start.4 = (bf16[544,128]{1,0:T(8,128)(2,1)S(1)}, bf16[544,128]{1,0:T(8,128)(2,1)S(1)}, u32[]{:S(2)}, u32[]{:S(2)}) collective-permute-start(bf16[544,128]{1,0:T(8,128)(2,1)S(1)} %get-tuple-element.36.refs_3_.refs_4_), channel_id=1, source_target_pairs={{0,1},{1,0},{2,3},{3,2},{4,5},{5,4},{6,7},{7,6},{8,9},{9,8},{10,11... | collective-permute-start | bytes 417800 | tf_op jit(solution)/shard_map/ppermute | solution.py:676
  18.3 1.1 %collective-permute-start.5 = (bf16[544,128]{1,0:T(8,128)(2,1)S(1)}, bf16[544,128]{1,0:T(8,128)(2,1)S(1)}, u32[]{:S(2)}, u32[]{:S(2)}) collective-permute-start(bf16[544,128]{1,0:T(8,128)(2,1)S(1)} %get-tuple-element.36.refs_3_.refs_4_), channel_id=1, source_target_pairs={{0,2},{1,3},{2,0},{3,1},{4,6},{5,7},{6,4},{7,5},{8,10},{9,11},{10,... | collective-permute-start | bytes 417800 | tf_op jit(solution)/shard_map/ppermute | solution.py:676
  19.5 0.7 %collective-permute-start.8 = (f32[3,128,128]{2,1,0:T(8,128)S(1)}, f32[3,128,128]{2,1,0:T(8,128)S(1)}, u32[]{:S(2)}, u32[]{:S(2)}) collective-permute-start(f32[3,128,128]{2,1,0:T(8,128)S(1)} %pad_maximum_fusion.1), channel_id=1, source_target_pairs={{0,16},{16,0},{1,17},{17,1},{2,18},{18,2},{3,19},{19,3},{4,20},{20... | collective-permute-start | bytes 589832 | tf_op jit(solution)/shard_map/ppermute | solution.py:726
  20.2 0.1 concatenate.45.at_ref
  20.2 0.1 copy.10
  20.3 0.1 copy.11
  20.5 4.8 %collective-permute-done.4.refs_4_.refs_5_ = bf16[544,128]{1,0:T(8,128)(2,1)S(1)} collective-permute-done((bf16[544,128]{1,0:T(8,128)(2,1)S(1)}, bf16[544,128]{1,0:T(8,128)(2,1)S(1)}, u32[]{:S(2)}, u32[]{:S(2)}) %collective-permute-start.4) | collective-permute-done | bytes 139296 | tf_op jit(solution)/shard_map/ppermute | solution.py:676
  25.3 2.5 %collective-permute-done.5.refs_5_.refs_6_ = bf16[544,128]{1,0:T(8,128)(2,1)S(1)} collective-permute-done((bf16[544,128]{1,0:T(8,128)(2,1)S(1)}, bf16[544,128]{1,0:T(8,128)(2,1)S(1)}, u32[]{:S(2)}, u32[]{:S(2)}) %collective-permute-start.5) | collective-permute-done | bytes 139296 | tf_op jit(solution)/shard_map/ppermute | solution.py:676
  27.8 0.1 copy.12
  28.0 0.5 collective-permute-start.10
  28.5 2.5 %match.1.refs_8_ = f32[3,8,1024]{2,1,0:T(8,128)S(1)} custom-call(s32[14]{0:T(128)S(1)} %concatenate.45.at_ref, bf16[1040,128]{1,0:T(8,128)(2,1)S(1)} %query_payload.1.refs_0_, bf16[1040,128]{1,0:T(8,128)(2,1)S(1)} %collective-permute-done.2.refs_1_, bf16[1040,128]{1,0:T(8,128)(2,1)S(1)} %collective-permute-done.3.refs_2_, ...), custom_call_target="tpu_custom_call" | custom-call | flops 603979776 | bytes 147456 | tf_op jit(solution)/shard_map/match/pallas_call | solution.py:175
  31.0 3.0 %collective-permute-done.10.refs_7_ = bf16[544,128]{1,0:T(8,128)(2,1)S(1)} collective-permute-done((bf16[544,128]{1,0:T(8,128)(2,1)S(1)}, bf16[544,128]{1,0:T(8,128)(2,1)S(1)}, u32[]{:S(2)}, u32[]{:S(2)}) %collective-permute-start.10) | collective-permute-done | bytes 139296 | tf_op jit(solution)/shard_map/ppermute | solution.py:676
  34.1 3.4 %match_rest.1 = f32[2,4,56,128]{3,2,1,0:T(8,128)} custom-call(s32[14]{0:T(128)S(1)} %concatenate.45.at_ref, bf16[1040,128]{1,0:T(8,128)(2,1)S(1)} %query_payload.1.refs_0_, bf16[1040,128]{1,0:T(8,128)(2,1)S(1)} %collective-permute-done.2.refs_1_, bf16[1040,128]{1,0:T(8,128)(2,1)S(1)} %collective-permute-done.3.refs_2_, ...), custom_call_target="tpu_custom_call" | custom-call | flops 469762048 | bytes 114688 | tf_op jit(solution)/shard_map/match_rest/pallas_call | solution.py:175
  37.4 3.4 %all-to-all-start = ((f32[8,56,128]{2,1,0:T(8,128)}), f32[8,56,128]{2,1,0:T(8,128)S(1)}, u32[]{:S(2)}, u32[]{:S(2)}) async-start(f32[8,56,128]{2,1,0:T(8,128)} %bitcast.17), calls=%async_computation | async-start | bytes 458752 | tf_op jit(solution)/shard_map/all_to_all | solution.py:33
  40.9 5.7 %all-to-all-done.parts_ref = f32[8,56,128]{2,1,0:T(8,128)S(1)} async-done(((f32[8,56,128]{2,1,0:T(8,128)}), f32[8,56,128]{2,1,0:T(8,128)S(1)}, u32[]{:S(2)}, u32[]{:S(2)}) %all-to-all-start) | async-done | bytes 229408 | tf_op jit(solution)/shard_map/all_to_all | solution.py:33
  46.6 0.7 %combine.1 = f32[32,8,128]{2,1,0:T(8,128)} custom-call(f32[8,56,128]{2,1,0:T(8,128)S(1)} %all-to-all-done.parts_ref, f32[8,128]{1,0:T(8,128)S(1)} %get-tuple-element.40.place_ref), custom_call_target="tpu_custom_call" | custom-call | tf_op jit(solution)/shard_map/combine/pallas_call | solution.py:229
  47.4 0.1 copy.15
  47.5 2.7 %all-to-all-start.1 = ((f32[32,8,128]{2,1,0:T(8,128)}), f32[32,8,128]{2,1,0:T(8,128)S(1)}, u32[]{:S(2)}, u32[]{:S(2)}) async-start(f32[32,8,128]{2,1,0:T(8,128)} %combine.1), calls=%async_computation.1 | async-start | bytes 262144 | tf_op jit(solution)/shard_map/all_to_all | solution.py:33
  50.3 0.1 maximum_maximum_fusion
  50.4 2.3 %spots.1 = (s32[1]{0:T(128)}, s32[16,8,128]{2,1,0:T(8,128)S(1)}, s32[16,2,8,128]{3,2,1,0:T(8,128)S(1)}, f32[144,256]{1,0:T(8,128)S(1)}) custom-call(s32[14]{0:T(128)S(1)} %concatenate.45.at_ref, f32[2,4,56,128]{3,2,1,0:T(8,128)S(1)} %bitcast.50), custom_call_target="tpu_custom_call" | custom-call | flops 301989888 | bytes 458752 | tf_op jit(solution)/shard_map/spots/pallas_call | solution.py:326
  52.6 0.2 slice.100
  52.8 0.2 pad_maximum_fusion.mesh_ref
  53.0 5.7 %all-to-all-done.1 = f32[32,8,128]{2,1,0:T(8,128)S(1)} async-done(((f32[32,8,128]{2,1,0:T(8,128)}), f32[32,8,128]{2,1,0:T(8,128)S(1)}, u32[]{:S(2)}, u32[]{:S(2)}) %all-to-all-start.1) | async-done | bytes 131104 | tf_op jit(solution)/shard_map/all_to_all | solution.py:33
  58.7 4.5 %relax.1 = f32[2,128,128]{2,1,0:T(8,128)} custom-call(s32[14]{0:T(128)S(1)} %concatenate.45.at_ref, s32[1]{0:T(128)} %get-tuple-element.44.rounds_ref, s32[16,8,128]{2,1,0:T(8,128)S(1)} %get-tuple-element.45.rank_ref, s32[16,2,8,128]{3,2,1,0:T(8,128)S(1)} %get-tuple-element.46.spot_ref, f32[144,256]{1,0:T(8,128)S(1)} %get-tuple-element.47.count_ref, ...), custom_call_target="tpu_custom_call" | custom-call | tf_op jit(solution)/shard_map/relax/pallas_call | solution.py:787
  (37 shorter events, 0.6 us)
Async XLA Ops:
  0.7 6.8 %copy-start.2 = (f32[1,2,128,128]{3,2,1,0:T(8,128)S(1)}, f32[1,2,128,128]{3,2,1,0:T(8,128)}, u32[]{:S(2)}) copy-start(f32[1,2,128,128]{3,2,1,0:T(8,128)} %param.12) | copy-start | bytes 393220
  0.7 6.8 %copy-start.3 = (f32[1,128,128]{2,1,0:T(8,128)S(1)}, f32[1,128,128]{2,1,0:T(8,128)}, u32[]{:S(2)}) copy-start(f32[1,128,128]{2,1,0:T(8,128)} %param.13) | copy-start | bytes 196612
  2.5 11.1 %collective-permute-start = (bf16[576,128]{1,0:T(8,128)(2,1)}, bf16[576,128]{1,0:T(8,128)(2,1)S(1)}, u32[]{:S(2)}, u32[]{:S(2)}) collective-permute-start(bf16[576,128]{1,0:T(8,128)(2,1)} %get-tuple-element.28.first_ref), channel_id=1, source_target_pairs={{0,16},{16,0},{1,17},{17,1},{2,18},{18,2},{3,19},{19,3},{4,20},{20... | collective-permute-start | bytes 442376 | tf_op jit(solution)/shard_map/ppermute | solution.py:716
  5.5 8.1 %collective-permute-start.1 = (bf16[512,128]{1,0:T(8,128)(2,1)}, bf16[512,128]{1,0:T(8,128)(2,1)S(1)}, u32[]{:S(2)}, u32[]{:S(2)}) collective-permute-start(bf16[512,128]{1,0:T(8,128)(2,1)} %get-tuple-element.29.second_ref), channel_id=1, source_target_pairs={{0,16},{1,17},{2,18},{3,19},{4,20},{5,21},{6,22},{7,23},{8,24},{9,... | collective-permute-start | bytes 393224 | tf_op jit(solution)/shard_map/ppermute | solution.py:29
  7.6 10.8 %collective-permute-start.6 = (f32[3,4,128]{1,2,0:T(8,128)S(1)}, f32[3,4,128]{1,2,0:T(8,128)S(1)}, u32[]{:S(2)}, u32[]{:S(2)}) collective-permute-start(f32[3,4,128]{1,2,0:T(8,128)S(1)} %get-tuple-element.55), channel_id=1, source_target_pairs={{1,0},{2,1},{3,2},{5,4},{6,5},{7,6},{9,8},{10,9},{11,10},{13,12},{... | collective-permute-start | bytes 18440 | tf_op jit(solution)/shard_map/ppermute | solution.py:29
  8.9 10.6 %collective-permute-start.7 = (f32[3,4,128]{1,2,0:T(8,128)S(1)}, f32[3,4,128]{1,2,0:T(8,128)S(1)}, u32[]{:S(2)}, u32[]{:S(2)}) collective-permute-start(f32[3,4,128]{1,2,0:T(8,128)S(1)} %get-tuple-element.56), channel_id=1, source_target_pairs={{0,1},{1,2},{2,3},{4,5},{5,6},{6,7},{8,9},{9,10},{10,11},{12,13},{... | collective-permute-start | bytes 18440 | tf_op jit(solution)/shard_map/ppermute | solution.py:29
  13.5 0.9 %copy-start = (bf16[576,128]{1,0:T(8,128)(2,1)S(1)}, bf16[576,128]{1,0:T(8,128)(2,1)}, u32[]{:S(2)}) copy-start(bf16[576,128]{1,0:T(8,128)(2,1)} %get-tuple-element.28.first_ref) | copy-start | bytes 442372
  13.5 1.0 %copy-start.1 = (bf16[512,128]{1,0:T(8,128)(2,1)S(1)}, bf16[512,128]{1,0:T(8,128)(2,1)}, u32[]{:S(2)}) copy-start(bf16[512,128]{1,0:T(8,128)(2,1)} %get-tuple-element.29.second_ref) | copy-start | bytes 393220
  14.6 13.2 %collective-permute-start.2 = (bf16[1040,128]{1,0:T(8,128)(2,1)S(1)}, bf16[1040,128]{1,0:T(8,128)(2,1)S(1)}, u32[]{:S(2)}, u32[]{:S(2)}) collective-permute-start(bf16[1040,128]{1,0:T(8,128)(2,1)S(1)} %query_payload.1.refs_0_), channel_id=1, source_target_pairs={{0,4},{4,0},{8,12},{12,8},{1,5},{5,1},{9,13},{13,9},{2,6},{6,2},{1... | collective-permute-start | bytes 798728 | tf_op jit(solution)/shard_map/ppermute | solution.py:676
  14.6 13.1 %collective-permute-start.3 = (bf16[1040,128]{1,0:T(8,128)(2,1)S(1)}, bf16[1040,128]{1,0:T(8,128)(2,1)S(1)}, u32[]{:S(2)}, u32[]{:S(2)}) collective-permute-start(bf16[1040,128]{1,0:T(8,128)(2,1)S(1)} %query_payload.1.refs_0_), channel_id=1, source_target_pairs={{0,8},{4,12},{8,0},{12,4},{1,9},{5,13},{9,1},{13,5},{2,10},{6,14},... | collective-permute-start | bytes 798728 | tf_op jit(solution)/shard_map/ppermute | solution.py:676
  16.7 8.6 %collective-permute-start.4 = (bf16[544,128]{1,0:T(8,128)(2,1)S(1)}, bf16[544,128]{1,0:T(8,128)(2,1)S(1)}, u32[]{:S(2)}, u32[]{:S(2)}) collective-permute-start(bf16[544,128]{1,0:T(8,128)(2,1)S(1)} %get-tuple-element.36.refs_3_.refs_4_), channel_id=1, source_target_pairs={{0,1},{1,0},{2,3},{3,2},{4,5},{5,4},{6,7},{7,6},{8,9},{9,8},{10,11... | collective-permute-start | bytes 417800 | tf_op jit(solution)/shard_map/ppermute | solution.py:676
  18.3 9.4 %collective-permute-start.5 = (bf16[544,128]{1,0:T(8,128)(2,1)S(1)}, bf16[544,128]{1,0:T(8,128)(2,1)S(1)}, u32[]{:S(2)}, u32[]{:S(2)}) collective-permute-start(bf16[544,128]{1,0:T(8,128)(2,1)S(1)} %get-tuple-element.36.refs_3_.refs_4_), channel_id=1, source_target_pairs={{0,2},{1,3},{2,0},{3,1},{4,6},{5,7},{6,4},{7,5},{8,10},{9,11},{10,... | collective-permute-start | bytes 417800 | tf_op jit(solution)/shard_map/ppermute | solution.py:676
  19.5 8.3 %collective-permute-start.8 = (f32[3,128,128]{2,1,0:T(8,128)S(1)}, f32[3,128,128]{2,1,0:T(8,128)S(1)}, u32[]{:S(2)}, u32[]{:S(2)}) collective-permute-start(f32[3,128,128]{2,1,0:T(8,128)S(1)} %pad_maximum_fusion.1), channel_id=1, source_target_pairs={{0,16},{16,0},{1,17},{17,1},{2,18},{18,2},{3,19},{19,3},{4,20},{20... | collective-permute-start | bytes 589832 | tf_op jit(solution)/shard_map/ppermute | solution.py:726
  27.9 6.2 %collective-permute-start.9 = (bf16[1040,128]{1,0:T(8,128)(2,1)S(1)}, bf16[1040,128]{1,0:T(8,128)(2,1)S(1)}, u32[]{:S(2)}, u32[]{:S(2)}) collective-permute-start(bf16[1040,128]{1,0:T(8,128)(2,1)S(1)} %collective-permute-done.3.refs_2_), channel_id=1, source_target_pairs={{0,4},{4,0},{8,12},{12,8},{1,5},{5,1},{9,13},{13,9},{2,6},{6,2},{1... | collective-permute-start | bytes 798728 | tf_op jit(solution)/shard_map/ppermute | solution.py:676
  28.0 6.1 %collective-permute-start.10 = (bf16[544,128]{1,0:T(8,128)(2,1)S(1)}, bf16[544,128]{1,0:T(8,128)(2,1)S(1)}, u32[]{:S(2)}, u32[]{:S(2)}) collective-permute-start(bf16[544,128]{1,0:T(8,128)(2,1)S(1)} %collective-permute-done.5.refs_5_.refs_6_), channel_id=1, source_target_pairs={{0,1},{1,0},{2,3},{3,2},{4,5},{5,4},{6,7},{7,6},{8,9},{9,8},{10,11... | collective-permute-start | bytes 417800 | tf_op jit(solution)/shard_map/ppermute | solution.py:676
  37.4 9.2 %all-to-all-start = ((f32[8,56,128]{2,1,0:T(8,128)}), f32[8,56,128]{2,1,0:T(8,128)S(1)}, u32[]{:S(2)}, u32[]{:S(2)}) async-start(f32[8,56,128]{2,1,0:T(8,128)} %bitcast.17), calls=%async_computation | async-start | bytes 458752 | tf_op jit(solution)/shard_map/all_to_all | solution.py:33
  47.5 11.1 %all-to-all-start.1 = ((f32[32,8,128]{2,1,0:T(8,128)}), f32[32,8,128]{2,1,0:T(8,128)S(1)}, u32[]{:S(2)}, u32[]{:S(2)}) async-start(f32[32,8,128]{2,1,0:T(8,128)} %combine.1), calls=%async_computation.1 | async-start | bytes 262144 | tf_op jit(solution)/shard_map/all_to_all | solution.py:33
where the time goes:
time: 64 us; the launch traced here: 63.2 us
  starting transfers between devices  23.1 us (36%)
  waiting for transfers between devices  21.6 us (34%)
  Pallas kernels  15.3 us (24%)
  local copies, waits for them, and re-layouts  1.74 us (3%)
  between operations  0.98 us (2%)
    all_to_all x2, waiting for transfers between devices, exchanged(): return lax.all_to_all(value, axes, split_axis=0, concat_axis=0, tiled=True)  11.3 us
    ppermute x6, waiting for transfers between devices, gathered(): held[i][at] = lax.ppermute(held[i][at ^ by], axis, pairs)  10.3 us
    ppermute x3, starting transfers between devices, passed_along(): return lax.ppermute(value, axis, pairs)  7.85 us
    all_to_all x2, starting transfers between devices, exchanged(): return lax.all_to_all(value, axes, split_axis=0, concat_axis=0, tiled=True)  6.13 us
    pallas_call x2, Pallas kernels, call(): pl.pallas_call(functools.partial(match_kernel, score_factor * math.log2(m...  5.88 us
    ppermute x6, starting transfers between devices, gathered(): held[i][at] = lax.ppermute(held[i][at ^ by], axis, pairs)  5.42 us
    pallas_call x1, Pallas kernels, per_device(): pl.pallas_call(functools.partial(relax_kernel, side, halo, extent), out_s...  4.53 us
    ppermute x1, starting transfers between devices, per_device(): other = lax.ppermute(first_half, 'sec', swap)  3 us
  transfers between devices with their start and end apart: 13, of which 5 were waited for; matrix products, arithmetic and copies ran while one was open for 2% of the time, Pallas kernels for 8%

commit v1 on v0

--- a/solution.py
+++ b/solution.py
@@ -13,7 +13,7 @@
 LANES = 128
 PLACE_ROWS = 16
 GROUP = 2
-ROUND = 8
+ROUND = 4
 BASE = 256
 DIGITS = 3
 VMEM_BYTES = 24 * 1024 * 1024

time: 64 us -> 65.3 us (1.020)
  Pallas kernels: 15.3 us -> 16.8 us
  waiting for transfers between devices: 21.6 us -> 20.8 us
  starting transfers between devices: 23.1 us -> 23.9 us
    pallas_call x2, Pallas kernels: 5.88 us -> 6.73 us  [call(): pl.pallas_call(functools.partial(match_kernel, score_factor * math.log2(m...]
    ppermute x6, waiting for transfers between devices: 10.3 us -> 9.44 us  [gathered(): held[i][at] = lax.ppermute(held[i][at ^ by], axis, pairs)]
    all_to_all x2, starting transfers between devices: 6.13 us -> 6.98 us  [exchanged(): return lax.all_to_all(value, axes, split_axis=0, concat_axis=0, tiled=True)]
  transfers between devices with their start and end apart: 13 -> 13, of which waited for: 5 -> 5; matrix products, arithmetic and copies ran while one was open for 2% -> 1% of each run, Pallas kernels for 8% -> 9%
where the time goes in v1:
time: 65.3 us; the launch traced here: 64.7 us
  starting transfers between devices  23.9 us (37%)
  waiting for transfers between devices  20.8 us (32%)
  Pallas kernels  16.8 us (26%)
  local copies, waits for them, and re-layouts  1.74 us (3%)
  between operations  0.98 us (2%)
    all_to_all x2, waiting for transfers between devices, exchanged(): return lax.all_to_all(value, axes, split_axis=0, concat_axis=0, tiled=True)  11.3 us
    ppermute x6, waiting for transfers between devices, gathered(): held[i][at] = lax.ppermute(held[i][at ^ by], axis, pairs)  9.44 us
    ppermute x3, starting transfers between devices, passed_along(): return lax.ppermute(value, axis, pairs)  7.85 us
    all_to_all x2, starting transfers between devices, exchanged(): return lax.all_to_all(value, axes, split_axis=0, concat_axis=0, tiled=True)  6.98 us
    pallas_call x2, Pallas kernels, call(): pl.pallas_call(functools.partial(match_kernel, score_factor * math.log2(m...  6.73 us
    ppermute x6, starting transfers between devices, gathered(): held[i][at] = lax.ppermute(held[i][at ^ by], axis, pairs)  5.42 us
    pallas_call x1, Pallas kernels, per_device(): pl.pallas_call(functools.partial(relax_kernel, side, halo, extent), out_s...  4.93 us
    ppermute x1, starting transfers between devices, per_device(): other = lax.ppermute(first_half, 'sec', swap)  3 us
  transfers between devices with their start and end apart: 13, of which 5 were waited for; matrix products, arithmetic and copies ran while one was open for 1% of the time, Pallas kernels for 9%

profile of v1, /device:TPU:0, one launch (start us, length us, event | category | flops | bytes accessed | tf_op | source)
XLA Modules:
  0.0 64.7 jit_solution(1903705911850465418)
XLA Ops:
  0.7 1.8 %pack.1 = (bf16[576,128]{1,0:T(8,128)(2,1)}, bf16[512,128]{1,0:T(8,128)(2,1)}) custom-call(bf16[1024,128]{1,0:T(8,128)(2,1)} %bitcast.58, bf16[2,1024]{1,0:T(2,128)(2,1)} %bitcast.64, s32[1,1024]{1,0:T(1,128)} %bitcast.65, s32[1,32]{1,0:T(1,128)} %bitcast.66, s32[1,1]{1,0:T(1,128)} %bitcast.48.count_hbm), custom_call_target="tpu_custom_call" | custom-call | tf_op jit(solution)/shard_map/pack/pallas_call | solution.py:550
  2.5 3.0 %collective-permute-start = (bf16[576,128]{1,0:T(8,128)(2,1)}, bf16[576,128]{1,0:T(8,128)(2,1)S(1)}, u32[]{:S(2)}, u32[]{:S(2)}) collective-permute-start(bf16[576,128]{1,0:T(8,128)(2,1)} %get-tuple-element.28.first_ref), channel_id=1, source_target_pairs={{0,16},{16,0},{1,17},{17,1},{2,18},{18,2},{3,19},{19,3},{4,20},{20... | collective-permute-start | bytes 442376 | tf_op jit(solution)/shard_map/ppermute | solution.py:716
  5.5 1.9 %collective-permute-start.1 = (bf16[512,128]{1,0:T(8,128)(2,1)}, bf16[512,128]{1,0:T(8,128)(2,1)S(1)}, u32[]{:S(2)}, u32[]{:S(2)}) collective-permute-start(bf16[512,128]{1,0:T(8,128)(2,1)} %get-tuple-element.29.second_ref), channel_id=1, source_target_pairs={{0,16},{1,17},{2,18},{3,19},{4,20},{5,21},{6,22},{7,23},{8,24},{9,... | collective-permute-start | bytes 393224 | tf_op jit(solution)/shard_map/ppermute | solution.py:29
  7.4 0.1 fusion.1
  7.6 1.3 %collective-permute-start.6 = (f32[3,4,128]{1,2,0:T(8,128)S(1)}, f32[3,4,128]{1,2,0:T(8,128)S(1)}, u32[]{:S(2)}, u32[]{:S(2)}) collective-permute-start(f32[3,4,128]{1,2,0:T(8,128)S(1)} %get-tuple-element.55), channel_id=1, source_target_pairs={{1,0},{2,1},{3,2},{5,4},{6,5},{7,6},{9,8},{10,9},{11,10},{13,12},{... | collective-permute-start | bytes 18440 | tf_op jit(solution)/shard_map/ppermute | solution.py:29
  8.9 4.6 %collective-permute-start.7 = (f32[3,4,128]{1,2,0:T(8,128)S(1)}, f32[3,4,128]{1,2,0:T(8,128)S(1)}, u32[]{:S(2)}, u32[]{:S(2)}) collective-permute-start(f32[3,4,128]{1,2,0:T(8,128)S(1)} %get-tuple-element.56), channel_id=1, source_target_pairs={{0,1},{1,2},{2,3},{4,5},{5,6},{6,7},{8,9},{9,10},{10,11},{12,13},{... | collective-permute-start | bytes 18440 | tf_op jit(solution)/shard_map/ppermute | solution.py:29
  13.6 0.8 %copy-done = bf16[576,128]{1,0:T(8,128)(2,1)S(1)} copy-done((bf16[576,128]{1,0:T(8,128)(2,1)S(1)}, bf16[576,128]{1,0:T(8,128)(2,1)}, u32[]{:S(2)}) %copy-start) | copy-done | bytes 147480
  14.6 2.0 %collective-permute-start.3 = (bf16[1040,128]{1,0:T(8,128)(2,1)S(1)}, bf16[1040,128]{1,0:T(8,128)(2,1)S(1)}, u32[]{:S(2)}, u32[]{:S(2)}) collective-permute-start(bf16[1040,128]{1,0:T(8,128)(2,1)S(1)} %query_payload.1.refs_0_), channel_id=1, source_target_pairs={{0,8},{4,12},{8,0},{12,4},{1,9},{5,13},{9,1},{13,5},{2,10},{6,14},... | collective-permute-start | bytes 798728 | tf_op jit(solution)/shard_map/ppermute | solution.py:676
  16.7 1.6 %collective-permute-start.4 = (bf16[544,128]{1,0:T(8,128)(2,1)S(1)}, bf16[544,128]{1,0:T(8,128)(2,1)S(1)}, u32[]{:S(2)}, u32[]{:S(2)}) collective-permute-start(bf16[544,128]{1,0:T(8,128)(2,1)S(1)} %get-tuple-element.36.refs_3_.refs_4_), channel_id=1, source_target_pairs={{0,1},{1,0},{2,3},{3,2},{4,5},{5,4},{6,7},{7,6},{8,9},{9,8},{10,11... | collective-permute-start | bytes 417800 | tf_op jit(solution)/shard_map/ppermute | solution.py:676
  18.3 1.1 %collective-permute-start.5 = (bf16[544,128]{1,0:T(8,128)(2,1)S(1)}, bf16[544,128]{1,0:T(8,128)(2,1)S(1)}, u32[]{:S(2)}, u32[]{:S(2)}) collective-permute-start(bf16[544,128]{1,0:T(8,128)(2,1)S(1)} %get-tuple-element.36.refs_3_.refs_4_), channel_id=1, source_target_pairs={{0,2},{1,3},{2,0},{3,1},{4,6},{5,7},{6,4},{7,5},{8,10},{9,11},{10,... | collective-permute-start | bytes 417800 | tf_op jit(solution)/shard_map/ppermute | solution.py:676
  19.5 0.7 %collective-permute-start.8 = (f32[3,128,128]{2,1,0:T(8,128)S(1)}, f32[3,128,128]{2,1,0:T(8,128)S(1)}, u32[]{:S(2)}, u32[]{:S(2)}) collective-permute-start(f32[3,128,128]{2,1,0:T(8,128)S(1)} %pad_maximum_fusion.1), channel_id=1, source_target_pairs={{0,16},{16,0},{1,17},{17,1},{2,18},{18,2},{3,19},{19,3},{4,20},{20... | collective-permute-start | bytes 589832 | tf_op jit(solution)/shard_map/ppermute | solution.py:726
  20.2 0.1 concatenate.45.at_ref
  20.2 0.1 copy.10
  20.3 0.1 copy.11
  20.5 4.8 %collective-permute-done.4.refs_4_.refs_5_ = bf16[544,128]{1,0:T(8,128)(2,1)S(1)} collective-permute-done((bf16[544,128]{1,0:T(8,128)(2,1)S(1)}, bf16[544,128]{1,0:T(8,128)(2,1)S(1)}, u32[]{:S(2)}, u32[]{:S(2)}) %collective-permute-start.4) | collective-permute-done | bytes 139296 | tf_op jit(solution)/shard_map/ppermute | solution.py:676
  25.3 2.5 %collective-permute-done.5.refs_5_.refs_6_ = bf16[544,128]{1,0:T(8,128)(2,1)S(1)} collective-permute-done((bf16[544,128]{1,0:T(8,128)(2,1)S(1)}, bf16[544,128]{1,0:T(8,128)(2,1)S(1)}, u32[]{:S(2)}, u32[]{:S(2)}) %collective-permute-start.5) | collective-permute-done | bytes 139296 | tf_op jit(solution)/shard_map/ppermute | solution.py:676
  27.8 0.1 copy.12
  28.0 0.5 collective-permute-start.10
  28.5 3.4 %match.1.refs_8_ = f32[3,8,1024]{2,1,0:T(8,128)S(1)} custom-call(s32[14]{0:T(128)S(1)} %concatenate.45.at_ref, bf16[1040,128]{1,0:T(8,128)(2,1)S(1)} %query_payload.1.refs_0_, bf16[1040,128]{1,0:T(8,128)(2,1)S(1)} %collective-permute-done.2.refs_1_, bf16[1040,128]{1,0:T(8,128)(2,1)S(1)} %collective-permute-done.3.refs_2_, ...), custom_call_target="tpu_custom_call" | custom-call | flops 603979776 | bytes 147456 | tf_op jit(solution)/shard_map/match/pallas_call | solution.py:175
  31.9 2.2 %collective-permute-done.10.refs_7_ = bf16[544,128]{1,0:T(8,128)(2,1)S(1)} collective-permute-done((bf16[544,128]{1,0:T(8,128)(2,1)S(1)}, bf16[544,128]{1,0:T(8,128)(2,1)S(1)}, u32[]{:S(2)}, u32[]{:S(2)}) %collective-permute-start.10) | collective-permute-done | bytes 139296 | tf_op jit(solution)/shard_map/ppermute | solution.py:676
  34.1 3.4 %match_rest.1 = f32[2,4,56,128]{3,2,1,0:T(8,128)} custom-call(s32[14]{0:T(128)S(1)} %concatenate.45.at_ref, bf16[1040,128]{1,0:T(8,128)(2,1)S(1)} %query_payload.1.refs_0_, bf16[1040,128]{1,0:T(8,128)(2,1)S(1)} %collective-permute-done.2.refs_1_, bf16[1040,128]{1,0:T(8,128)(2,1)S(1)} %collective-permute-done.3.refs_2_, ...), custom_call_target="tpu_custom_call" | custom-call | flops 469762048 | bytes 114688 | tf_op jit(solution)/shard_map/match_rest/pallas_call | solution.py:175
  37.4 3.4 %all-to-all-start = ((f32[8,56,128]{2,1,0:T(8,128)}), f32[8,56,128]{2,1,0:T(8,128)S(1)}, u32[]{:S(2)}, u32[]{:S(2)}) async-start(f32[8,56,128]{2,1,0:T(8,128)} %bitcast.17), calls=%async_computation | async-start | bytes 458752 | tf_op jit(solution)/shard_map/all_to_all | solution.py:33
  40.9 0.1 pad.10.clone
  40.9 5.7 %all-to-all-done.parts_ref = f32[8,56,128]{2,1,0:T(8,128)S(1)} async-done(((f32[8,56,128]{2,1,0:T(8,128)}), f32[8,56,128]{2,1,0:T(8,128)S(1)}, u32[]{:S(2)}, u32[]{:S(2)}) %all-to-all-start) | async-done | bytes 229408 | tf_op jit(solution)/shard_map/all_to_all | solution.py:33
  46.6 0.7 %combine.1 = f32[32,8,128]{2,1,0:T(8,128)} custom-call(f32[8,56,128]{2,1,0:T(8,128)S(1)} %all-to-all-done.parts_ref, f32[8,128]{1,0:T(8,128)S(1)} %get-tuple-element.40.place_ref), custom_call_target="tpu_custom_call" | custom-call | tf_op jit(solution)/shard_map/combine/pallas_call | solution.py:229
  47.4 0.1 copy.15
  47.6 0.2 slice.100
  47.8 3.6 %all-to-all-start.1 = ((f32[32,8,128]{2,1,0:T(8,128)}), f32[32,8,128]{2,1,0:T(8,128)S(1)}, u32[]{:S(2)}, u32[]{:S(2)}) async-start(f32[32,8,128]{2,1,0:T(8,128)} %combine.1), calls=%async_computation.1 | async-start | bytes 262144 | tf_op jit(solution)/shard_map/all_to_all | solution.py:33
  51.4 2.5 %spots.1 = (s32[1]{0:T(128)}, s32[16,8,128]{2,1,0:T(8,128)S(1)}, s32[32,2,4,128]{3,2,1,0:T(4,128)S(1)}, f32[144,256]{1,0:T(8,128)S(1)}) custom-call(s32[14]{0:T(128)S(1)} %concatenate.45.at_ref, f32[2,4,56,128]{3,2,1,0:T(8,128)S(1)} %bitcast.50), custom_call_target="tpu_custom_call" | custom-call | flops 150994944 | bytes 458752 | tf_op jit(solution)/shard_map/spots/pallas_call | solution.py:326
  53.9 0.2 pad_maximum_fusion.mesh_ref
  54.1 5.7 %all-to-all-done.1 = f32[32,8,128]{2,1,0:T(8,128)S(1)} async-done(((f32[32,8,128]{2,1,0:T(8,128)}), f32[32,8,128]{2,1,0:T(8,128)S(1)}, u32[]{:S(2)}, u32[]{:S(2)}) %all-to-all-start.1) | async-done | bytes 131104 | tf_op jit(solution)/shard_map/all_to_all | solution.py:33
  59.8 4.9 %relax.1 = f32[2,128,128]{2,1,0:T(8,128)} custom-call(s32[14]{0:T(128)S(1)} %concatenate.45.at_ref, s32[1]{0:T(128)} %get-tuple-element.44.rounds_ref, s32[16,8,128]{2,1,0:T(8,128)S(1)} %get-tuple-element.45.rank_ref, s32[32,2,4,128]{3,2,1,0:T(4,128)S(1)} %get-tuple-element.46.spot_ref, f32[144,256]{1,0:T(8,128)S(1)} %get-tuple-element.47.count_ref, ...), custom_call_target="tpu_custom_call" | custom-call | tf_op jit(solution)/shard_map/relax/pallas_call | solution.py:787
  (37 shorter events, 0.6 us)
Async XLA Ops:
  0.7 6.8 %copy-start.2 = (f32[1,2,128,128]{3,2,1,0:T(8,128)S(1)}, f32[1,2,128,128]{3,2,1,0:T(8,128)}, u32[]{:S(2)}) copy-start(f32[1,2,128,128]{3,2,1,0:T(8,128)} %param.12) | copy-start | bytes 393220
  0.7 6.8 %copy-start.3 = (f32[1,128,128]{2,1,0:T(8,128)S(1)}, f32[1,128,128]{2,1,0:T(8,128)}, u32[]{:S(2)}) copy-start(f32[1,128,128]{2,1,0:T(8,128)} %param.13) | copy-start | bytes 196612
  2.5 11.1 %collective-permute-start = (bf16[576,128]{1,0:T(8,128)(2,1)}, bf16[576,128]{1,0:T(8,128)(2,1)S(1)}, u32[]{:S(2)}, u32[]{:S(2)}) collective-permute-start(bf16[576,128]{1,0:T(8,128)(2,1)} %get-tuple-element.28.first_ref), channel_id=1, source_target_pairs={{0,16},{16,0},{1,17},{17,1},{2,18},{18,2},{3,19},{19,3},{4,20},{20... | collective-permute-start | bytes 442376 | tf_op jit(solution)/shard_map/ppermute | solution.py:716
  5.5 8.1 %collective-permute-start.1 = (bf16[512,128]{1,0:T(8,128)(2,1)}, bf16[512,128]{1,0:T(8,128)(2,1)S(1)}, u32[]{:S(2)}, u32[]{:S(2)}) collective-permute-start(bf16[512,128]{1,0:T(8,128)(2,1)} %get-tuple-element.29.second_ref), channel_id=1, source_target_pairs={{0,16},{1,17},{2,18},{3,19},{4,20},{5,21},{6,22},{7,23},{8,24},{9,... | collective-permute-start | bytes 393224 | tf_op jit(solution)/shard_map/ppermute | solution.py:29
  7.6 10.8 %collective-permute-start.6 = (f32[3,4,128]{1,2,0:T(8,128)S(1)}, f32[3,4,128]{1,2,0:T(8,128)S(1)}, u32[]{:S(2)}, u32[]{:S(2)}) collective-permute-start(f32[3,4,128]{1,2,0:T(8,128)S(1)} %get-tuple-element.55), channel_id=1, source_target_pairs={{1,0},{2,1},{3,2},{5,4},{6,5},{7,6},{9,8},{10,9},{11,10},{13,12},{... | collective-permute-start | bytes 18440 | tf_op jit(solution)/shard_map/ppermute | solution.py:29
  8.9 10.6 %collective-permute-start.7 = (f32[3,4,128]{1,2,0:T(8,128)S(1)}, f32[3,4,128]{1,2,0:T(8,128)S(1)}, u32[]{:S(2)}, u32[]{:S(2)}) collective-permute-start(f32[3,4,128]{1,2,0:T(8,128)S(1)} %get-tuple-element.56), channel_id=1, source_target_pairs={{0,1},{1,2},{2,3},{4,5},{5,6},{6,7},{8,9},{9,10},{10,11},{12,13},{... | collective-permute-start | bytes 18440 | tf_op jit(solution)/shard_map/ppermute | solution.py:29
  13.5 0.9 %copy-start = (bf16[576,128]{1,0:T(8,128)(2,1)S(1)}, bf16[576,128]{1,0:T(8,128)(2,1)}, u32[]{:S(2)}) copy-start(bf16[576,128]{1,0:T(8,128)(2,1)} %get-tuple-element.28.first_ref) | copy-start | bytes 442372
  13.5 1.0 %copy-start.1 = (bf16[512,128]{1,0:T(8,128)(2,1)S(1)}, bf16[512,128]{1,0:T(8,128)(2,1)}, u32[]{:S(2)}) copy-start(bf16[512,128]{1,0:T(8,128)(2,1)} %get-tuple-element.29.second_ref) | copy-start | bytes 393220
  14.6 13.2 %collective-permute-start.2 = (bf16[1040,128]{1,0:T(8,128)(2,1)S(1)}, bf16[1040,128]{1,0:T(8,128)(2,1)S(1)}, u32[]{:S(2)}, u32[]{:S(2)}) collective-permute-start(bf16[1040,128]{1,0:T(8,128)(2,1)S(1)} %query_payload.1.refs_0_), channel_id=1, source_target_pairs={{0,4},{4,0},{8,12},{12,8},{1,5},{5,1},{9,13},{13,9},{2,6},{6,2},{1... | collective-permute-start | bytes 798728 | tf_op jit(solution)/shard_map/ppermute | solution.py:676
  14.6 13.1 %collective-permute-start.3 = (bf16[1040,128]{1,0:T(8,128)(2,1)S(1)}, bf16[1040,128]{1,0:T(8,128)(2,1)S(1)}, u32[]{:S(2)}, u32[]{:S(2)}) collective-permute-start(bf16[1040,128]{1,0:T(8,128)(2,1)S(1)} %query_payload.1.refs_0_), channel_id=1, source_target_pairs={{0,8},{4,12},{8,0},{12,4},{1,9},{5,13},{9,1},{13,5},{2,10},{6,14},... | collective-permute-start | bytes 798728 | tf_op jit(solution)/shard_map/ppermute | solution.py:676
  16.7 8.6 %collective-permute-start.4 = (bf16[544,128]{1,0:T(8,128)(2,1)S(1)}, bf16[544,128]{1,0:T(8,128)(2,1)S(1)}, u32[]{:S(2)}, u32[]{:S(2)}) collective-permute-start(bf16[544,128]{1,0:T(8,128)(2,1)S(1)} %get-tuple-element.36.refs_3_.refs_4_), channel_id=1, source_target_pairs={{0,1},{1,0},{2,3},{3,2},{4,5},{5,4},{6,7},{7,6},{8,9},{9,8},{10,11... | collective-permute-start | bytes 417800 | tf_op jit(solution)/shard_map/ppermute | solution.py:676
  18.3 9.4 %collective-permute-start.5 = (bf16[544,128]{1,0:T(8,128)(2,1)S(1)}, bf16[544,128]{1,0:T(8,128)(2,1)S(1)}, u32[]{:S(2)}, u32[]{:S(2)}) collective-permute-start(bf16[544,128]{1,0:T(8,128)(2,1)S(1)} %get-tuple-element.36.refs_3_.refs_4_), channel_id=1, source_target_pairs={{0,2},{1,3},{2,0},{3,1},{4,6},{5,7},{6,4},{7,5},{8,10},{9,11},{10,... | collective-permute-start | bytes 417800 | tf_op jit(solution)/shard_map/ppermute | solution.py:676
  19.5 8.3 %collective-permute-start.8 = (f32[3,128,128]{2,1,0:T(8,128)S(1)}, f32[3,128,128]{2,1,0:T(8,128)S(1)}, u32[]{:S(2)}, u32[]{:S(2)}) collective-permute-start(f32[3,128,128]{2,1,0:T(8,128)S(1)} %pad_maximum_fusion.1), channel_id=1, source_target_pairs={{0,16},{16,0},{1,17},{17,1},{2,18},{18,2},{3,19},{19,3},{4,20},{20... | collective-permute-start | bytes 589832 | tf_op jit(solution)/shard_map/ppermute | solution.py:726
  27.9 6.2 %collective-permute-start.9 = (bf16[1040,128]{1,0:T(8,128)(2,1)S(1)}, bf16[1040,128]{1,0:T(8,128)(2,1)S(1)}, u32[]{:S(2)}, u32[]{:S(2)}) collective-permute-start(bf16[1040,128]{1,0:T(8,128)(2,1)S(1)} %collective-permute-done.3.refs_2_), channel_id=1, source_target_pairs={{0,4},{4,0},{8,12},{12,8},{1,5},{5,1},{9,13},{13,9},{2,6},{6,2},{1... | collective-permute-start | bytes 798728 | tf_op jit(solution)/shard_map/ppermute | solution.py:676
  28.0 6.1 %collective-permute-start.10 = (bf16[544,128]{1,0:T(8,128)(2,1)S(1)}, bf16[544,128]{1,0:T(8,128)(2,1)S(1)}, u32[]{:S(2)}, u32[]{:S(2)}) collective-permute-start(bf16[544,128]{1,0:T(8,128)(2,1)S(1)} %collective-permute-done.5.refs_5_.refs_6_), channel_id=1, source_target_pairs={{0,1},{1,0},{2,3},{3,2},{4,5},{5,4},{6,7},{7,6},{8,9},{9,8},{10,11... | collective-permute-start | bytes 417800 | tf_op jit(solution)/shard_map/ppermute | solution.py:676
  37.4 9.2 %all-to-all-start = ((f32[8,56,128]{2,1,0:T(8,128)}), f32[8,56,128]{2,1,0:T(8,128)S(1)}, u32[]{:S(2)}, u32[]{:S(2)}) async-start(f32[8,56,128]{2,1,0:T(8,128)} %bitcast.17), calls=%async_computation | async-start | bytes 458752 | tf_op jit(solution)/shard_map/all_to_all | solution.py:33
  47.8 12.0 %all-to-all-start.1 = ((f32[32,8,128]{2,1,0:T(8,128)}), f32[32,8,128]{2,1,0:T(8,128)S(1)}, u32[]{:S(2)}, u32[]{:S(2)}) async-start(f32[32,8,128]{2,1,0:T(8,128)} %combine.1), calls=%async_computation.1 | async-start | bytes 262144 | tf_op jit(solution)/shard_map/all_to_all | solution.py:33

commit v2 on v1

--- a/solution.py
+++ b/solution.py
@@ -13,7 +13,7 @@
 LANES = 128
 PLACE_ROWS = 16
 GROUP = 2
-ROUND = 4
+ROUND = 24
 BASE = 256
 DIGITS = 3
 VMEM_BYTES = 24 * 1024 * 1024

time: 65.3 us -> 64.4 us (0.986)
  starting transfers between devices: 23.9 us -> 23 us
    all_to_all x2, starting transfers between devices: 6.98 us -> 6 us  [exchanged(): return lax.all_to_all(value, axes, split_axis=0, concat_axis=0, tiled=True)]
    pallas_call x2, Pallas kernels: 6.73 us -> 7.58 us  [call(): pl.pallas_call(functools.partial(match_kernel, score_factor * math.log2(m...]
  transfers between devices with their start and end apart: 13 -> 13, of which waited for: 5 -> 5; matrix products, arithmetic and copies ran while one was open for 1% -> 2% of each run, Pallas kernels for 9% -> 9%
where the time goes in v2:
time: 64.4 us; the launch traced here: 64.1 us
  starting transfers between devices  23 us (36%)
  waiting for transfers between devices  20.7 us (32%)
  Pallas kernels  17.3 us (27%)
  local copies, waits for them, and re-layouts  1.74 us (3%)
  between operations  0.98 us (2%)
    all_to_all x2, waiting for transfers between devices, exchanged(): return lax.all_to_all(value, axes, split_axis=0, concat_axis=0, tiled=True)  11.3 us
    ppermute x6, waiting for transfers between devices, gathered(): held[i][at] = lax.ppermute(held[i][at ^ by], axis, pairs)  9.44 us
    ppermute x3, starting transfers between devices, passed_along(): return lax.ppermute(value, axis, pairs)  7.85 us
    pallas_call x2, Pallas kernels, call(): pl.pallas_call(functools.partial(match_kernel, score_factor * math.log2(m...  7.58 us
    all_to_all x2, starting transfers between devices, exchanged(): return lax.all_to_all(value, axes, split_axis=0, concat_axis=0, tiled=True)  6 us
    ppermute x6, starting transfers between devices, gathered(): held[i][at] = lax.ppermute(held[i][at ^ by], axis, pairs)  5.42 us
    pallas_call x1, Pallas kernels, per_device(): pl.pallas_call(functools.partial(relax_kernel, side, halo, extent), out_s...  4.72 us
    ppermute x1, starting transfers between devices, per_device(): other = lax.ppermute(first_half, 'sec', swap)  3 us
  transfers between devices with their start and end apart: 13, of which 5 were waited for; matrix products, arithmetic and copies ran while one was open for 2% of the time, Pallas kernels for 9%

profile of v2, /device:TPU:0, one launch (start us, length us, event | category | flops | bytes accessed | tf_op | source)
XLA Modules:
  0.0 64.1 jit_solution(7019267310912006794)
XLA Ops:
  0.7 1.8 %pack.1 = (bf16[576,128]{1,0:T(8,128)(2,1)}, bf16[512,128]{1,0:T(8,128)(2,1)}) custom-call(bf16[1024,128]{1,0:T(8,128)(2,1)} %bitcast.58, bf16[2,1024]{1,0:T(2,128)(2,1)} %bitcast.64, s32[1,1024]{1,0:T(1,128)} %bitcast.65, s32[1,32]{1,0:T(1,128)} %bitcast.66, s32[1,1]{1,0:T(1,128)} %bitcast.48.count_hbm), custom_call_target="tpu_custom_call" | custom-call | tf_op jit(solution)/shard_map/pack/pallas_call | solution.py:550
  2.5 3.0 %collective-permute-start = (bf16[576,128]{1,0:T(8,128)(2,1)}, bf16[576,128]{1,0:T(8,128)(2,1)S(1)}, u32[]{:S(2)}, u32[]{:S(2)}) collective-permute-start(bf16[576,128]{1,0:T(8,128)(2,1)} %get-tuple-element.28.first_ref), channel_id=1, source_target_pairs={{0,16},{16,0},{1,17},{17,1},{2,18},{18,2},{3,19},{19,3},{4,20},{20... | collective-permute-start | bytes 442376 | tf_op jit(solution)/shard_map/ppermute | solution.py:716
  5.5 1.9 %collective-permute-start.1 = (bf16[512,128]{1,0:T(8,128)(2,1)}, bf16[512,128]{1,0:T(8,128)(2,1)S(1)}, u32[]{:S(2)}, u32[]{:S(2)}) collective-permute-start(bf16[512,128]{1,0:T(8,128)(2,1)} %get-tuple-element.29.second_ref), channel_id=1, source_target_pairs={{0,16},{1,17},{2,18},{3,19},{4,20},{5,21},{6,22},{7,23},{8,24},{9,... | collective-permute-start | bytes 393224 | tf_op jit(solution)/shard_map/ppermute | solution.py:29
  7.4 0.1 fusion.1
  7.6 1.3 %collective-permute-start.6 = (f32[3,4,128]{1,2,0:T(8,128)S(1)}, f32[3,4,128]{1,2,0:T(8,128)S(1)}, u32[]{:S(2)}, u32[]{:S(2)}) collective-permute-start(f32[3,4,128]{1,2,0:T(8,128)S(1)} %get-tuple-element.55), channel_id=1, source_target_pairs={{1,0},{2,1},{3,2},{5,4},{6,5},{7,6},{9,8},{10,9},{11,10},{13,12},{... | collective-permute-start | bytes 18440 | tf_op jit(solution)/shard_map/ppermute | solution.py:29
  8.9 4.6 %collective-permute-start.7 = (f32[3,4,128]{1,2,0:T(8,128)S(1)}, f32[3,4,128]{1,2,0:T(8,128)S(1)}, u32[]{:S(2)}, u32[]{:S(2)}) collective-permute-start(f32[3,4,128]{1,2,0:T(8,128)S(1)} %get-tuple-element.56), channel_id=1, source_target_pairs={{0,1},{1,2},{2,3},{4,5},{5,6},{6,7},{8,9},{9,10},{10,11},{12,13},{... | collective-permute-start | bytes 18440 | tf_op jit(solution)/shard_map/ppermute | solution.py:29
  13.6 0.8 %copy-done = bf16[576,128]{1,0:T(8,128)(2,1)S(1)} copy-done((bf16[576,128]{1,0:T(8,128)(2,1)S(1)}, bf16[576,128]{1,0:T(8,128)(2,1)}, u32[]{:S(2)}) %copy-start) | copy-done | bytes 147480
  14.6 2.0 %collective-permute-start.3 = (bf16[1040,128]{1,0:T(8,128)(2,1)S(1)}, bf16[1040,128]{1,0:T(8,128)(2,1)S(1)}, u32[]{:S(2)}, u32[]{:S(2)}) collective-permute-start(bf16[1040,128]{1,0:T(8,128)(2,1)S(1)} %query_payload.1.refs_0_), channel_id=1, source_target_pairs={{0,8},{4,12},{8,0},{12,4},{1,9},{5,13},{9,1},{13,5},{2,10},{6,14},... | collective-permute-start | bytes 798728 | tf_op jit(solution)/shard_map/ppermute | solution.py:676
  16.7 1.6 %collective-permute-start.4 = (bf16[544,128]{1,0:T(8,128)(2,1)S(1)}, bf16[544,128]{1,0:T(8,128)(2,1)S(1)}, u32[]{:S(2)}, u32[]{:S(2)}) collective-permute-start(bf16[544,128]{1,0:T(8,128)(2,1)S(1)} %get-tuple-element.36.refs_3_.refs_4_), channel_id=1, source_target_pairs={{0,1},{1,0},{2,3},{3,2},{4,5},{5,4},{6,7},{7,6},{8,9},{9,8},{10,11... | collective-permute-start | bytes 417800 | tf_op jit(solution)/shard_map/ppermute | solution.py:676
  18.3 1.1 %collective-permute-start.5 = (bf16[544,128]{1,0:T(8,128)(2,1)S(1)}, bf16[544,128]{1,0:T(8,128)(2,1)S(1)}, u32[]{:S(2)}, u32[]{:S(2)}) collective-permute-start(bf16[544,128]{1,0:T(8,128)(2,1)S(1)} %get-tuple-element.36.refs_3_.refs_4_), channel_id=1, source_target_pairs={{0,2},{1,3},{2,0},{3,1},{4,6},{5,7},{6,4},{7,5},{8,10},{9,11},{10,... | collective-permute-start | bytes 417800 | tf_op jit(solution)/shard_map/ppermute | solution.py:676
  19.5 0.7 %collective-permute-start.8 = (f32[3,128,128]{2,1,0:T(8,128)S(1)}, f32[3,128,128]{2,1,0:T(8,128)S(1)}, u32[]{:S(2)}, u32[]{:S(2)}) collective-permute-start(f32[3,128,128]{2,1,0:T(8,128)S(1)} %pad_maximum_fusion.1), channel_id=1, source_target_pairs={{0,16},{16,0},{1,17},{17,1},{2,18},{18,2},{3,19},{19,3},{4,20},{20... | collective-permute-start | bytes 589832 | tf_op jit(solution)/shard_map/ppermute | solution.py:726
  20.2 0.1 concatenate.45.at_ref
  20.2 0.1 copy.10
  20.3 0.1 copy.11
  20.5 4.8 %collective-permute-done.4.refs_4_.refs_5_ = bf16[544,128]{1,0:T(8,128)(2,1)S(1)} collective-permute-done((bf16[544,128]{1,0:T(8,128)(2,1)S(1)}, bf16[544,128]{1,0:T(8,128)(2,1)S(1)}, u32[]{:S(2)}, u32[]{:S(2)}) %collective-permute-start.4) | collective-permute-done | bytes 139296 | tf_op jit(solution)/shard_map/ppermute | solution.py:676
  25.3 2.5 %collective-permute-done.5.refs_5_.refs_6_ = bf16[544,128]{1,0:T(8,128)(2,1)S(1)} collective-permute-done((bf16[544,128]{1,0:T(8,128)(2,1)S(1)}, bf16[544,128]{1,0:T(8,128)(2,1)S(1)}, u32[]{:S(2)}, u32[]{:S(2)}) %collective-permute-start.5) | collective-permute-done | bytes 139296 | tf_op jit(solution)/shard_map/ppermute | solution.py:676
  27.8 0.1 copy.12
  28.0 0.5 collective-permute-start.10
  28.5 3.4 %match.1.refs_8_ = f32[3,8,1024]{2,1,0:T(8,128)S(1)} custom-call(s32[14]{0:T(128)S(1)} %concatenate.45.at_ref, bf16[1040,128]{1,0:T(8,128)(2,1)S(1)} %query_payload.1.refs_0_, bf16[1040,128]{1,0:T(8,128)(2,1)S(1)} %collective-permute-done.2.refs_1_, bf16[1040,128]{1,0:T(8,128)(2,1)S(1)} %collective-permute-done.3.refs_2_, ...), custom_call_target="tpu_custom_call" | custom-call | flops 603979776 | bytes 147456 | tf_op jit(solution)/shard_map/match/pallas_call | solution.py:175
  31.9 2.2 %collective-permute-done.10.refs_7_ = bf16[544,128]{1,0:T(8,128)(2,1)S(1)} collective-permute-done((bf16[544,128]{1,0:T(8,128)(2,1)S(1)}, bf16[544,128]{1,0:T(8,128)(2,1)S(1)}, u32[]{:S(2)}, u32[]{:S(2)}) %collective-permute-start.10) | collective-permute-done | bytes 139296 | tf_op jit(solution)/shard_map/ppermute | solution.py:676
  34.1 4.2 %match_rest.1 = f32[2,4,56,128]{3,2,1,0:T(8,128)} custom-call(s32[14]{0:T(128)S(1)} %concatenate.45.at_ref, bf16[1040,128]{1,0:T(8,128)(2,1)S(1)} %query_payload.1.refs_0_, bf16[1040,128]{1,0:T(8,128)(2,1)S(1)} %collective-permute-done.2.refs_1_, bf16[1040,128]{1,0:T(8,128)(2,1)S(1)} %collective-permute-done.3.refs_2_, ...), custom_call_target="tpu_custom_call" | custom-call | flops 469762048 | bytes 114688 | tf_op jit(solution)/shard_map/match_rest/pallas_call | solution.py:175
  38.3 3.4 %all-to-all-start = ((f32[8,56,128]{2,1,0:T(8,128)}), f32[8,56,128]{2,1,0:T(8,128)S(1)}, u32[]{:S(2)}, u32[]{:S(2)}) async-start(f32[8,56,128]{2,1,0:T(8,128)} %bitcast.17), calls=%async_computation | async-start | bytes 458752 | tf_op jit(solution)/shard_map/all_to_all | solution.py:33
  41.8 5.7 %all-to-all-done.parts_ref = f32[8,56,128]{2,1,0:T(8,128)S(1)} async-done(((f32[8,56,128]{2,1,0:T(8,128)}), f32[8,56,128]{2,1,0:T(8,128)S(1)}, u32[]{:S(2)}, u32[]{:S(2)}) %all-to-all-start) | async-done | bytes 229408 | tf_op jit(solution)/shard_map/all_to_all | solution.py:33
  47.4 0.7 %combine.1 = f32[32,8,128]{2,1,0:T(8,128)} custom-call(f32[8,56,128]{2,1,0:T(8,128)S(1)} %all-to-all-done.parts_ref, f32[8,128]{1,0:T(8,128)S(1)} %get-tuple-element.40.place_ref), custom_call_target="tpu_custom_call" | custom-call | tf_op jit(solution)/shard_map/combine/pallas_call | solution.py:229
  48.3 0.1 copy.15
  48.4 2.6 %all-to-all-start.1 = ((f32[32,8,128]{2,1,0:T(8,128)}), f32[32,8,128]{2,1,0:T(8,128)S(1)}, u32[]{:S(2)}, u32[]{:S(2)}) async-start(f32[32,8,128]{2,1,0:T(8,128)} %combine.1), calls=%async_computation.1 | async-start | bytes 262144 | tf_op jit(solution)/shard_map/all_to_all | solution.py:33
  51.0 0.1 maximum_maximum_fusion
  51.1 2.3 %spots.1 = (s32[1]{0:T(128)}, s32[16,8,128]{2,1,0:T(8,128)S(1)}, s32[6,2,24,128]{3,2,1,0:T(8,128)S(1)}, f32[144,256]{1,0:T(8,128)S(1)}) custom-call(s32[14]{0:T(128)S(1)} %concatenate.45.at_ref, f32[2,4,56,128]{3,2,1,0:T(8,128)S(1)} %bitcast.50), custom_call_target="tpu_custom_call" | custom-call | flops 905969664 | bytes 458752 | tf_op jit(solution)/shard_map/spots/pallas_call | solution.py:326
  53.4 0.2 slice.100
  53.6 0.2 pad_maximum_fusion.mesh_ref
  53.8 5.6 %all-to-all-done.1 = f32[32,8,128]{2,1,0:T(8,128)S(1)} async-done(((f32[32,8,128]{2,1,0:T(8,128)}), f32[32,8,128]{2,1,0:T(8,128)S(1)}, u32[]{:S(2)}, u32[]{:S(2)}) %all-to-all-start.1) | async-done | bytes 131104 | tf_op jit(solution)/shard_map/all_to_all | solution.py:33
  59.4 4.7 %relax.1 = f32[2,128,128]{2,1,0:T(8,128)} custom-call(s32[14]{0:T(128)S(1)} %concatenate.45.at_ref, s32[1]{0:T(128)} %get-tuple-element.44.rounds_ref, s32[16,8,128]{2,1,0:T(8,128)S(1)} %get-tuple-element.45.rank_ref, s32[6,2,24,128]{3,2,1,0:T(8,128)S(1)} %get-tuple-element.46.spot_ref, f32[144,256]{1,0:T(8,128)S(1)} %get-tuple-element.47.count_ref, ...), custom_call_target="tpu_custom_call" | custom-call | tf_op jit(solution)/shard_map/relax/pallas_call | solution.py:787
  (37 shorter events, 0.6 us)
Async XLA Ops:
  0.7 6.8 %copy-start.2 = (f32[1,2,128,128]{3,2,1,0:T(8,128)S(1)}, f32[1,2,128,128]{3,2,1,0:T(8,128)}, u32[]{:S(2)}) copy-start(f32[1,2,128,128]{3,2,1,0:T(8,128)} %param.12) | copy-start | bytes 393220
  0.7 6.8 %copy-start.3 = (f32[1,128,128]{2,1,0:T(8,128)S(1)}, f32[1,128,128]{2,1,0:T(8,128)}, u32[]{:S(2)}) copy-start(f32[1,128,128]{2,1,0:T(8,128)} %param.13) | copy-start | bytes 196612
  2.5 11.1 %collective-permute-start = (bf16[576,128]{1,0:T(8,128)(2,1)}, bf16[576,128]{1,0:T(8,128)(2,1)S(1)}, u32[]{:S(2)}, u32[]{:S(2)}) collective-permute-start(bf16[576,128]{1,0:T(8,128)(2,1)} %get-tuple-element.28.first_ref), channel_id=1, source_target_pairs={{0,16},{16,0},{1,17},{17,1},{2,18},{18,2},{3,19},{19,3},{4,20},{20... | collective-permute-start | bytes 442376 | tf_op jit(solution)/shard_map/ppermute | solution.py:716
  5.5 8.1 %collective-permute-start.1 = (bf16[512,128]{1,0:T(8,128)(2,1)}, bf16[512,128]{1,0:T(8,128)(2,1)S(1)}, u32[]{:S(2)}, u32[]{:S(2)}) collective-permute-start(bf16[512,128]{1,0:T(8,128)(2,1)} %get-tuple-element.29.second_ref), channel_id=1, source_target_pairs={{0,16},{1,17},{2,18},{3,19},{4,20},{5,21},{6,22},{7,23},{8,24},{9,... | collective-permute-start | bytes 393224 | tf_op jit(solution)/shard_map/ppermute | solution.py:29
  7.6 10.8 %collective-permute-start.6 = (f32[3,4,128]{1,2,0:T(8,128)S(1)}, f32[3,4,128]{1,2,0:T(8,128)S(1)}, u32[]{:S(2)}, u32[]{:S(2)}) collective-permute-start(f32[3,4,128]{1,2,0:T(8,128)S(1)} %get-tuple-element.55), channel_id=1, source_target_pairs={{1,0},{2,1},{3,2},{5,4},{6,5},{7,6},{9,8},{10,9},{11,10},{13,12},{... | collective-permute-start | bytes 18440 | tf_op jit(solution)/shard_map/ppermute | solution.py:29
  8.9 10.6 %collective-permute-start.7 = (f32[3,4,128]{1,2,0:T(8,128)S(1)}, f32[3,4,128]{1,2,0:T(8,128)S(1)}, u32[]{:S(2)}, u32[]{:S(2)}) collective-permute-start(f32[3,4,128]{1,2,0:T(8,128)S(1)} %get-tuple-element.56), channel_id=1, source_target_pairs={{0,1},{1,2},{2,3},{4,5},{5,6},{6,7},{8,9},{9,10},{10,11},{12,13},{... | collective-permute-start | bytes 18440 | tf_op jit(solution)/shard_map/ppermute | solution.py:29
  13.5 0.9 %copy-start = (bf16[576,128]{1,0:T(8,128)(2,1)S(1)}, bf16[576,128]{1,0:T(8,128)(2,1)}, u32[]{:S(2)}) copy-start(bf16[576,128]{1,0:T(8,128)(2,1)} %get-tuple-element.28.first_ref) | copy-start | bytes 442372
  13.5 1.0 %copy-start.1 = (bf16[512,128]{1,0:T(8,128)(2,1)S(1)}, bf16[512,128]{1,0:T(8,128)(2,1)}, u32[]{:S(2)}) copy-start(bf16[512,128]{1,0:T(8,128)(2,1)} %get-tuple-element.29.second_ref) | copy-start | bytes 393220
  14.6 13.2 %collective-permute-start.2 = (bf16[1040,128]{1,0:T(8,128)(2,1)S(1)}, bf16[1040,128]{1,0:T(8,128)(2,1)S(1)}, u32[]{:S(2)}, u32[]{:S(2)}) collective-permute-start(bf16[1040,128]{1,0:T(8,128)(2,1)S(1)} %query_payload.1.refs_0_), channel_id=1, source_target_pairs={{0,4},{4,0},{8,12},{12,8},{1,5},{5,1},{9,13},{13,9},{2,6},{6,2},{1... | collective-permute-start | bytes 798728 | tf_op jit(solution)/shard_map/ppermute | solution.py:676
  14.6 13.1 %collective-permute-start.3 = (bf16[1040,128]{1,0:T(8,128)(2,1)S(1)}, bf16[1040,128]{1,0:T(8,128)(2,1)S(1)}, u32[]{:S(2)}, u32[]{:S(2)}) collective-permute-start(bf16[1040,128]{1,0:T(8,128)(2,1)S(1)} %query_payload.1.refs_0_), channel_id=1, source_target_pairs={{0,8},{4,12},{8,0},{12,4},{1,9},{5,13},{9,1},{13,5},{2,10},{6,14},... | collective-permute-start | bytes 798728 | tf_op jit(solution)/shard_map/ppermute | solution.py:676
  16.7 8.6 %collective-permute-start.4 = (bf16[544,128]{1,0:T(8,128)(2,1)S(1)}, bf16[544,128]{1,0:T(8,128)(2,1)S(1)}, u32[]{:S(2)}, u32[]{:S(2)}) collective-permute-start(bf16[544,128]{1,0:T(8,128)(2,1)S(1)} %get-tuple-element.36.refs_3_.refs_4_), channel_id=1, source_target_pairs={{0,1},{1,0},{2,3},{3,2},{4,5},{5,4},{6,7},{7,6},{8,9},{9,8},{10,11... | collective-permute-start | bytes 417800 | tf_op jit(solution)/shard_map/ppermute | solution.py:676
  18.3 9.4 %collective-permute-start.5 = (bf16[544,128]{1,0:T(8,128)(2,1)S(1)}, bf16[544,128]{1,0:T(8,128)(2,1)S(1)}, u32[]{:S(2)}, u32[]{:S(2)}) collective-permute-start(bf16[544,128]{1,0:T(8,128)(2,1)S(1)} %get-tuple-element.36.refs_3_.refs_4_), channel_id=1, source_target_pairs={{0,2},{1,3},{2,0},{3,1},{4,6},{5,7},{6,4},{7,5},{8,10},{9,11},{10,... | collective-permute-start | bytes 417800 | tf_op jit(solution)/shard_map/ppermute | solution.py:676
  19.5 8.3 %collective-permute-start.8 = (f32[3,128,128]{2,1,0:T(8,128)S(1)}, f32[3,128,128]{2,1,0:T(8,128)S(1)}, u32[]{:S(2)}, u32[]{:S(2)}) collective-permute-start(f32[3,128,128]{2,1,0:T(8,128)S(1)} %pad_maximum_fusion.1), channel_id=1, source_target_pairs={{0,16},{16,0},{1,17},{17,1},{2,18},{18,2},{3,19},{19,3},{4,20},{20... | collective-permute-start | bytes 589832 | tf_op jit(solution)/shard_map/ppermute | solution.py:726
  27.9 6.2 %collective-permute-start.9 = (bf16[1040,128]{1,0:T(8,128)(2,1)S(1)}, bf16[1040,128]{1,0:T(8,128)(2,1)S(1)}, u32[]{:S(2)}, u32[]{:S(2)}) collective-permute-start(bf16[1040,128]{1,0:T(8,128)(2,1)S(1)} %collective-permute-done.3.refs_2_), channel_id=1, source_target_pairs={{0,4},{4,0},{8,12},{12,8},{1,5},{5,1},{9,13},{13,9},{2,6},{6,2},{1... | collective-permute-start | bytes 798728 | tf_op jit(solution)/shard_map/ppermute | solution.py:676
  28.0 6.1 %collective-permute-start.10 = (bf16[544,128]{1,0:T(8,128)(2,1)S(1)}, bf16[544,128]{1,0:T(8,128)(2,1)S(1)}, u32[]{:S(2)}, u32[]{:S(2)}) collective-permute-start(bf16[544,128]{1,0:T(8,128)(2,1)S(1)} %collective-permute-done.5.refs_5_.refs_6_), channel_id=1, source_target_pairs={{0,1},{1,0},{2,3},{3,2},{4,5},{5,4},{6,7},{7,6},{8,9},{9,8},{10,11... | collective-permute-start | bytes 417800 | tf_op jit(solution)/shard_map/ppermute | solution.py:676
  38.3 9.2 %all-to-all-start = ((f32[8,56,128]{2,1,0:T(8,128)}), f32[8,56,128]{2,1,0:T(8,128)S(1)}, u32[]{:S(2)}, u32[]{:S(2)}) async-start(f32[8,56,128]{2,1,0:T(8,128)} %bitcast.17), calls=%async_computation | async-start | bytes 458752 | tf_op jit(solution)/shard_map/all_to_all | solution.py:33
  48.4 11.0 %all-to-all-start.1 = ((f32[32,8,128]{2,1,0:T(8,128)}), f32[32,8,128]{2,1,0:T(8,128)S(1)}, u32[]{:S(2)}, u32[]{:S(2)}) async-start(f32[32,8,128]{2,1,0:T(8,128)} %combine.1), calls=%async_computation.1 | async-start | bytes 262144 | tf_op jit(solution)/shard_map/all_to_all | solution.py:33
